TPU v7x, 256 devices: a whole 4x4x8 slice. The times are simulated.
256 devices in a mesh: branch: 32 (over x, z), row: 4 (over y), top: 2 (over core).
Axes of the slice: x: 4, y: 4, z: 8, core: 2. Of those that a mesh axis runs over, the one named last changes fastest.
Arguments:
- right_sides: bfloat16 [16, 2097152], P(None, ('branch', 'row', 'top')), may hold values from -6 to 6
- positions: bfloat16 [3, 2097152], P(None, ('branch', 'row', 'top')), may hold values from -2 to 2
- point_order: int32 [2097152], P(('branch', 'row', 'top')), may hold values from 0 to 8191, as said below
- leaf_basis: bfloat16 [32, 2097152], P(None, ('branch', 'row', 'top')), may hold values from -0.75 to 0.75
- transfer: bfloat16 [65024, 1024], P(('branch', 'row', 'top')), may hold values from -0.75 to 0.75
- couple_local: bfloat16 [65024, 6, 1024], P(('branch', 'row', 'top')), may hold values from -0.4375 to 0.4375
- partner_local: int32 [65024, 6], P(('branch', 'row', 'top')), may hold values from 0 to 1023, as said below
- transfer_up: bfloat16 [496, 1024], replicated, may hold values from -0.75 to 0.75
- couple_up: bfloat16 [504, 6, 1024], P('top'), may hold values from -2 to 2
- partner_up: int32 [504, 6], replicated, may hold values from 0 to 503, as said below
- send_list: int32 [256, 8, 16], P(('branch', 'row', 'top')), may hold values from 0 to 127, as said below
- side_list: int32 [256, 2, 32], P(('branch', 'row', 'top')), may hold values from 0 to 127, as said below
- pair_target: int32 [256, 1024], P(('branch', 'row', 'top')), may hold values from 0 to 127, as said below
- pair_source: int32 [256, 1024], P(('branch', 'row', 'top')), may hold values from 0 to 319
- pair_count: int32 [256], P(('branch', 'row', 'top')), may hold values from 192 to 1024, as said below
Outputs:
- potential: float32 [16, 2097152], P(None, ('branch', 'row', 'top'))
Inputs may be any that keep to these rules, and one draw needn't show every extreme that they name: `point_order`: each device's block of 8192 entries is a permutation of its own rows. `partner_local`: A node of level k has exactly 6 distinct partners, none itself, among the 8 * 128 / 2^k level-k nodes of its subtree, numbered member * 128 / 2^k + node. `partner_up`: an upper node has exactly 6 distinct partners, none itself, all of its own level. `send_list`: for each sender and member, 16 distinct leaves of the sender. `side_list`: for each sender and side, 32 distinct leaves of the sender. `pair_target`: local leaves of the device; entries at and beyond the device's count are ignored. `pair_count`: some device has the full 1024 pairs.
All inputs are finite; a program needn't handle non-finite values.
Results may differ from a plain program's by a relative error of at most 0.025.
Values may be sent and summed in bfloat16 or wider, within the bound.
A program may use at most 192 MiB of HBM per device.

v0:
```python
import jax
import jax.numpy as jnp
from jax import lax
from jax.experimental import pallas as pl
from jax.experimental.pallas import tpu as pltpu
from jax.sharding import PartitionSpec as P

LEAF = 64
RANK = 32
NRHS = 16
FAR = 6
SLOT = 16
HALO = 32
LEAVES = 128
POINTS = LEAVES * LEAF
NODES = 2 * LEAVES - 2
GROUP = 8
BRANCHES = 32
UPPER = 504
LEVELS = 7
TILES = 64

INV_FOUR_PI = 0.07957747154594767
SOFTENING = 0.01

BF = jnp.bfloat16
F32 = jnp.float32
I32 = jnp.int32
MESH = pl.DeviceIdType.MESH
VMEM = pl.BlockSpec(memory_space=pltpu.VMEM)
SMEM = pl.BlockSpec(memory_space=pltpu.SMEM)
ANY = pl.BlockSpec(memory_space=pl.ANY)


def dot(a, b):
    return jnp.dot(a, b, preferred_element_type=F32)


def dot_nt(a, b):
    return lax.dot_general(a, b, (((1,), (1,)), ((), ())), preferred_element_type=F32)


def iota(shape, axis):
    return lax.broadcasted_iota(I32, shape, axis)


def first_row(level):
    return 2 * LEAVES - 2 * (LEAVES >> level)


def block_turns(value):
    return [value] + [pltpu.roll(value, 32 * step, 1) for step in range(1, 4)]


def spread_edges(rows_of, put):
    value = rows_of(0)
    shape = value.shape
    owner = (iota(shape, 0) >> 1) & 3
    lane = iota(shape, 1) >> 5
    masks = [(owner == k) & (lane == k) for k in range(4)]
    for g in range(8):
        turns = block_turns(rows_of(g))
        for p in range(4):
            out = jnp.zeros(shape, F32)
            for k in range(4):
                out = jnp.where(masks[k], turns[(k - p) % 4], out)
            put(4 * g + p, out)


def spread_blocks(rows_of, put):
    lane = None
    for g in range(8):
        turns = [block_turns(rows_of(f, g)) for f in range(FAR)]
        if lane is None:
            lane = iota(turns[0][0].shape, 1) >> 5
        for a in range(4):
            pick = [turns[f][(f % 4 - a) % 4] for f in range(FAR)]
            low = jnp.where(
                lane == 0, pick[0], jnp.where(lane == 1, pick[1], jnp.where(lane == 2, pick[2], pick[3]))
            )
            high = jnp.where(lane == 0, pick[4], jnp.where(lane == 1, pick[5], 0.0))
            put(4 * g + a, low, high)


def stack_rows(rows, shape):
    sub = iota(shape, 0)
    out = jnp.zeros(shape, F32)
    for k, row in enumerate(rows):
        out = jnp.where(sub == k, row, out)
    return out


def split_three(value):
    high = value.astype(BF).astype(F32)
    rest = value - high
    middle = rest.astype(BF).astype(F32)
    return high, middle, rest - middle


def source_features(xyz):
    x, y, z = xyz[0:1], xyz[1:2], xyz[2:3]
    high, middle, low = split_three(x * x + y * y + z * z)
    return stack_rows([x, y, z, 1.0, 1.0, 1.0, high, middle, low], (16, xyz.shape[1]))


def target_features(xyz):
    x, y, z = xyz[0:1], xyz[1:2], xyz[2:3]
    high, middle, low = split_three(x * x + y * y + z * z + SOFTENING)
    return stack_rows(
        [-2.0 * x, -2.0 * y, -2.0 * z, high, middle, low, 1.0, 1.0, 1.0], (16, xyz.shape[1])
    )


def leaf_blocks(basis):
    lane = iota(basis.shape, 1) >> 6
    zero = jnp.zeros(basis.shape, basis.dtype)
    return jnp.concatenate([jnp.where(lane == j, basis, zero) for j in range(4)], axis=0)


def exchange_kernel(
    rhs, xyz, order, basis, trans, tup, cup, send_s, side_s,
    table_o, pool_o, upper_o, edges_o, edges_up_o, cup_o,
    x_s, table_s, pool_s, edge_s, tail_s, near_s, side_buf, root_s, roots_s, upper_s, cup_send, cup_recv,
    near_send, near_recv, pool_send, pool_recv, root_send, root_recv, up_send, up_recv, cup_sem, local_sem,
):
    branch = lax.axis_index("branch")
    row = lax.axis_index("row")
    top = lax.axis_index("top")
    me = row * 2 + top
    device = branch * GROUP + me

    def member(index):
        return (branch, index // 2, index % 2)

    def peer(offset):
        return (me + offset) % GROUP

    def cousin(offset):
        return ((branch + offset) % BRANCHES, row, top)

    barrier = pltpu.get_barrier_semaphore()
    for offset in range(1, GROUP):
        pl.semaphore_signal(barrier, inc=1, device_id=member(peer(offset)), device_id_type=MESH)

    def greet(offset, carry):
        pl.semaphore_signal(barrier, inc=1, device_id=cousin(offset), device_id_type=MESH)
        return carry

    lax.fori_loop(1, BRANCHES, greet, 0)

    for low in range(32):
        x_s[16 * low : 16 * low + 16, :] = rhs[:, 256 * low : 256 * low + 256]

    def chunk(c, carry):
        lanes = pl.ds(pl.multiple_of(c * 256, 256), 256)
        index = order[:, lanes]
        hot = (iota((256, 256), 0) == (index & 255)).astype(F32).astype(BF)
        wide = dot(x_s[...], hot)
        part = index >> 8
        ordered = jnp.zeros((16, 256), F32)
        for low in range(32):
            ordered = jnp.where(part == low, wide[16 * low : 16 * low + 16], ordered)
        features = source_features(xyz[:, lanes].astype(F32))
        left = iota((16, 128), 1) < 64
        for half in range(2):
            value = ordered[:, 128 * half : 128 * half + 128]
            extra = features[:, 128 * half : 128 * half + 128]
            table_s[4 * c + 2 * half] = jnp.where(left, value, pltpu.roll(extra, 64, 1)).astype(BF)
            table_s[4 * c + 2 * half + 1] = jnp.where(left, pltpu.roll(value, 64, 1), extra).astype(BF)
        pool_s[c] = dot_nt(ordered.astype(BF), leaf_blocks(basis[:, lanes])).astype(BF)
        return carry

    lax.fori_loop(0, 32, chunk, 0)

    def fill(k, carry):
        for m in range(GROUP):
            near_s[m, k] = table_s[send_s[m, k]]
        return carry

    lax.fori_loop(0, SLOT, fill, 0)

    def fill_side(k, carry):
        for s in range(2):
            side_buf[s, k] = table_s[side_s[s, k]]
        return carry

    lax.fori_loop(0, HALO, fill_side, 0)

    pl.semaphore_wait(barrier, GROUP - 1 + BRANCHES - 1)

    started = []

    def send(src, dst, send_sem, recv_sem, device_id):
        copy = pltpu.make_async_remote_copy(
            src_ref=src, dst_ref=dst, send_sem=send_sem, recv_sem=recv_sem,
            device_id=device_id, device_id_type=MESH,
        )
        copy.start()
        started.append(copy)

    locals_ = []

    def keep(src, dst, sem):
        copy = pltpu.make_async_copy(src, dst, sem)
        copy.start()
        locals_.append(copy)

    for offset in range(1, GROUP):
        send(
            pool_s.at[pl.ds(0, 32)], pool_o.at[me, pl.ds(0, 32)],
            pool_send.at[offset - 1], pool_recv.at[offset - 1], member(peer(offset)),
        )
    for offset in range(1, GROUP):
        send(
            near_s.at[peer(offset)], table_o.at[pl.ds(LEAVES + me * SLOT, SLOT)],
            near_send.at[offset - 1], near_recv.at[offset - 1], member(peer(offset)),
        )
    send(
        side_buf.at[1], table_o.at[pl.ds(2 * LEAVES, HALO)],
        near_send.at[7], near_recv.at[7], cousin(1),
    )
    send(
        side_buf.at[0], table_o.at[pl.ds(2 * LEAVES + HALO, HALO)],
        near_send.at[8], near_recv.at[8], cousin(BRANCHES - 1),
    )
    keep(table_s, table_o.at[pl.ds(0, LEAVES)], local_sem.at[0])
    keep(near_s.at[me], table_o.at[pl.ds(LEAVES + me * SLOT, SLOT)], local_sem.at[1])

    slot = iota((16, 252), 0)
    shape = slot & 7
    base = jnp.where(slot < 8, device, device + 1 - 2 * top)
    node = jnp.full((16, 252), -1, I32)
    for level in range(6):
        node = jnp.where(shape == level, 512 - (512 >> level) + (base >> level), node)
    hot = (iota((16, 252), 1) + 252 * top == node).astype(F32).astype(BF)
    for f in range(FAR):
        chosen = dot(hot, cup[f])
        cup_o[f] = chosen[0:8]
        cup_send[f] = chosen[8:16]
    send(cup_send, cup_recv, cup_sem.at[0], cup_sem.at[1], (branch, row, 1 - top))

    tail_s[...] = jnp.zeros((16, 1024), F32)
    tail_s[0:14, :] = trans[240:254, :].astype(F32)

    def spread(c, carry):
        start = pl.multiple_of(c * 16, 16)

        def put(p, out):
            edge_s[pl.ds(c * 512 + p, 16, stride=32), :] = out

        spread_edges(lambda g: trans[pl.ds(start, 16), 128 * g : 128 * g + 128].astype(F32), put)
        return carry

    lax.fori_loop(0, 15, spread, 0)

    def put_tail(p, out):
        edge_s[pl.ds(15 * 512 + p, 16, stride=32), :] = out

    spread_edges(lambda g: tail_s[:, 128 * g : 128 * g + 128], put_tail)

    def round_edges(c, carry):
        rows = pl.ds(pl.multiple_of(c * 256, 256), 256)
        edges_o[rows, :] = edge_s[rows, :].astype(BF)
        return carry

    lax.fori_loop(0, 32, round_edges, 0)

    tile_of = [first_row(level) // 4 for level in range(LEVELS)]
    for level in range(LEVELS - 2):
        for t in range((LEAVES >> level) // 8):
            child = tile_of[level] + 2 * t
            pair = jnp.concatenate([pool_s[child], pool_s[child + 1]], axis=1)
            rows = (first_row(level) + 8 * t) * 32
            pool_s[tile_of[level + 1] + t] = dot(pair, edges_o[rows : rows + 256, :]).astype(BF)
    rows = first_row(5) * 32
    pool_s[63] = dot(pool_s[62], edges_o[rows : rows + 128, :]).astype(BF)
    rows = first_row(6) * 32
    root = dot(pool_s[63], edges_o[rows : rows + 128, :])
    placed = root
    for k in (0, 1, 3):
        placed = jnp.where(me % 4 == k, pltpu.roll(root, (32 * (k - 2)) % 128, 1), placed)
    root_s[...] = placed.astype(BF)
    for offset in range(1, GROUP):
        send(
            root_s, roots_s.at[me],
            root_send.at[offset - 1], root_recv.at[offset - 1], member(peer(offset)),
        )
    roots_s[me] = root_s[...]
    roots = started[-7:]
    for offset in range(1, GROUP):
        send(
            pool_s.at[pl.ds(32, 32)], pool_o.at[me, pl.ds(32, 32)],
            pool_send.at[offset + 6], pool_recv.at[offset + 6], member(peer(offset)),
        )
    keep(pool_s, pool_o.at[me], local_sem.at[2])

    slot = iota((64, 496), 0)
    want = jnp.where(
        slot < 8,
        8 * branch + slot,
        jnp.where(
            slot < 12,
            248 + 4 * branch + slot,
            jnp.where(slot < 14, 372 + 2 * branch + slot, jnp.where(slot < 16, -1, 432 + slot)),
        ),
    )
    chosen = dot((iota((64, 496), 1) == want).astype(F32).astype(BF), tup[...])

    def put_up(p, out):
        edge_s[pl.ds(p, 64, stride=32), :] = out

    spread_edges(lambda g: chosen[:, 128 * g : 128 * g + 128], put_up)
    edges_up_o[...] = edge_s[0:2048, :].astype(BF)

    for copy in roots:
        copy.wait_recv()
    low = roots_s[0] + roots_s[1] + roots_s[2] + roots_s[3]
    high = roots_s[4] + roots_s[5] + roots_s[6] + roots_s[7]
    upper_s[0] = low
    upper_s[1] = high
    first = dot(jnp.concatenate([low, high], axis=1), edges_up_o[0:256, :]).astype(BF)
    upper_s[2] = first
    second = dot(first, edges_up_o[256:384, :]).astype(BF)
    third = dot(second[:, 0:64], edges_up_o[384:448, :]).astype(BF)
    upper_s[3] = jnp.where(iota((16, 128), 1) < 64, second.astype(F32), third.astype(F32)).astype(BF)

    def spread_up(offset, carry):
        pltpu.make_async_remote_copy(
            src_ref=upper_s, dst_ref=upper_o.at[branch],
            send_sem=up_send.at[offset - 1], recv_sem=up_recv.at[offset - 1],
            device_id=cousin(offset), device_id_type=MESH,
        ).start()
        return carry

    lax.fori_loop(1, BRANCHES, spread_up, 0)
    keep(upper_s, upper_o.at[branch], local_sem.at[3])

    for copy in started:
        copy.wait_send()
        if not any(copy is other for other in roots):
            copy.wait_recv()
    for copy in locals_:
        copy.wait()
    cup_o[...] = cup_o[...] + cup_recv[...]

    def finish(offset, carry):
        pltpu.make_async_remote_copy(
            src_ref=upper_s, dst_ref=upper_o.at[branch],
            send_sem=up_send.at[offset - 1], recv_sem=up_recv.at[offset - 1],
            device_id=cousin(offset), device_id_type=MESH,
        ).wait()
        return carry

    lax.fori_loop(1, BRANCHES, finish, 0)


def exchange(rhs, xyz, order, basis, trans, tup, cup, send_list, side_list):
    shape = jax.ShapeDtypeStruct
    return pl.pallas_call(
        exchange_kernel,
        out_shape=(
            shape((2 * LEAVES + 2 * HALO, 16, 128), BF),
            shape((GROUP, TILES, 16, 128), BF),
            shape((BRANCHES, 4, 16, 128), BF),
            shape((8192, 128), BF),
            shape((2048, 128), BF),
            shape((FAR, 8, 1024), F32),
        ),
        in_specs=[VMEM] * 7 + [SMEM] * 2,
        out_specs=(ANY, ANY, ANY, VMEM, VMEM, VMEM),
        scratch_shapes=[
            pltpu.VMEM((512, 256), BF),
            pltpu.VMEM((LEAVES, 16, 128), BF),
            pltpu.VMEM((TILES, 16, 128), BF),
            pltpu.VMEM((8192, 128), F32),
            pltpu.VMEM((16, 1024), F32),
            pltpu.VMEM((GROUP, SLOT, 16, 128), BF),
            pltpu.VMEM((2, HALO, 16, 128), BF),
            pltpu.VMEM((16, 128), BF),
            pltpu.VMEM((GROUP, 16, 128), BF),
            pltpu.VMEM((4, 16, 128), BF),
            pltpu.VMEM((FAR, 8, 1024), F32),
            pltpu.VMEM((FAR, 8, 1024), F32),
            pltpu.SemaphoreType.DMA((9,)),
            pltpu.SemaphoreType.DMA((9,)),
            pltpu.SemaphoreType.DMA((14,)),
            pltpu.SemaphoreType.DMA((14,)),
            pltpu.SemaphoreType.DMA((7,)),
            pltpu.SemaphoreType.DMA((7,)),
            pltpu.SemaphoreType.DMA((BRANCHES - 1,)),
            pltpu.SemaphoreType.DMA((BRANCHES - 1,)),
            pltpu.SemaphoreType.DMA((2,)),
            pltpu.SemaphoreType.DMA((4,)),
        ],
        compiler_params=pltpu.CompilerParams(
            collective_id=0, has_side_effects=True, vmem_limit_bytes=48 * 1024 * 1024
        ),
        name="exchange",
    )(rhs, xyz, order, basis, trans, tup, cup, send_list, side_list)


def local_kernel(
    order, basis, xyz, table, pool, upper, edges, edges_up, cup, couple, codes, pup, target, source, count,
    out,
    feat_s, goal_s, pool_rep, block_s, tail_s, block_up, upper_s, coupled_s, local_s, near_s, sum_s,
):
    branch = lax.axis_index("branch")
    me = lax.axis_index("row") * 2 + lax.axis_index("top")
    device = branch * GROUP + me
    left = iota((16, 128), 1) < 64
    lane_block = iota((16, 128), 1) >> 5

    def goals(c, carry):
        lanes = pl.ds(pl.multiple_of(c * 256, 256), 256)
        features = target_features(xyz[:, lanes].astype(F32))
        for half in range(2):
            value = features[:, 128 * half : 128 * half + 128]
            turned = pltpu.roll(value, 64, 1)
            goal_s[4 * c + 2 * half] = jnp.where(left, value, turned).astype(BF)
            goal_s[4 * c + 2 * half + 1] = jnp.where(left, turned, value).astype(BF)
        return carry

    lax.fori_loop(0, 32, goals, 0)

    eye = (iota((128, 128), 0) == iota((128, 128), 1)).astype(F32).astype(BF)

    def sources(c, carry):
        first = pltpu.roll(table[2 * c].astype(F32), 64, 1)
        both = jnp.where(left, first, table[2 * c + 1].astype(F32)).astype(BF)
        turned = dot_nt(eye, jnp.concatenate([both] * 8, axis=0)).astype(BF)
        feat_s[2 * c] = turned[0:64]
        feat_s[2 * c + 1] = turned[64:128]
        return carry

    lax.fori_loop(0, 160, sources, 0, unroll=4)

    def clear(t, carry):
        near_s[t] = jnp.zeros((16, 128), F32)
        return carry

    lax.fori_loop(0, LEAVES + 1, clear, 0, unroll=3)

    live = count[0]
    lane16 = (iota((64, 64), 1) >> 4)
    zero = jnp.zeros((16, 128), BF)

    def quad(first):
        at = [source[0, first + i] for i in range(4)]
        to = [target[0, first + i] for i in range(4)]
        f = [feat_s[at[i]][:, 0:64] for i in range(4)]
        lhs = jnp.where(lane16 == 0, f[0], jnp.where(lane16 == 1, f[1], jnp.where(lane16 == 2, f[2], f[3])))
        g = [goal_s[to[i]] for i in range(4)]
        rhs = jnp.concatenate(
            [
                jnp.concatenate([jnp.where(left, g[0], zero), zero], axis=1),
                jnp.concatenate([jnp.where(left, zero, g[1]), zero], axis=1),
                jnp.concatenate([zero, jnp.where(left, g[2], zero)], axis=1),
                jnp.concatenate([zero, jnp.where(left, zero, g[3])], axis=1),
            ],
            axis=0,
        )
        tile = lax.rsqrt(dot(lhs, rhs)).astype(BF)
        values = jnp.concatenate([table[at[i]][:, 0:64] for i in range(4)], axis=0)
        wide = dot(values, tile)
        outs = []
        for i in range(4):
            part = wide[16 * i : 16 * i + 16, 128 * (i // 2) : 128 * (i // 2) + 128]
            goal = jnp.where(first + i < live, to[i], LEAVES)
            outs.append((goal, jnp.where(left if i % 2 == 0 else ~left, part, 0.0)))
        return outs

    def near(c, carry):
        outs = []
        for k in range(4):
            outs += quad(c * 16 + 4 * k)
        for goal, part in outs:
            near_s[goal] = near_s[goal] + part
        return carry

    lax.fori_loop(0, (live + 15) // 16, near, 0)

    tail_s[...] = jnp.zeros((FAR, 16, 1024), F32)
    for f in range(FAR):
        tail_s[f, 0:14, :] = couple[f, 240:254, :].astype(F32)

    def spread(c, carry):
        start = pl.multiple_of(c * 16, 16)

        def put(a, low, high):
            block_s[0, pl.ds(c * 512 + a, 16, stride=32), :] = low
            block_s[1, pl.ds(c * 512 + a, 16, stride=32), :] = high

        spread_blocks(lambda f, g: couple[f, pl.ds(start, 16), 128 * g : 128 * g + 128].astype(F32), put)
        return carry

    lax.fori_loop(0, 15, spread, 0)

    def put_tail(a, low, high):
        block_s[0, pl.ds(15 * 512 + a, 16, stride=32), :] = low
        block_s[1, pl.ds(15 * 512 + a, 16, stride=32), :] = high

    spread_blocks(lambda f, g: tail_s[f, :, 128 * g : 128 * g + 128], put_tail)

    def put_up(a, low, high):
        block_up[0, pl.ds(a, 8, stride=32), :] = low
        block_up[1, pl.ds(a, 8, stride=32), :] = high

    spread_blocks(lambda f, g: cup[f, :, 128 * g : 128 * g + 128], put_up)

    def widen(t, carry):
        turns = [v.astype(BF) for v in block_turns(pool[t].astype(F32))]
        for j in range(4):
            value = turns[(3 - j) % 4]
            for k in range(3):
                value = jnp.where(lane_block == k, turns[(k - j) % 4], value)
            pool_rep[4 * t + j] = value
        return carry

    lax.fori_loop(0, GROUP * TILES, widen, 0, unroll=2)

    def picks_of(pick):
        low = jnp.where(
            lane_block == 0,
            pick[0],
            jnp.where(lane_block == 1, pick[1], jnp.where(lane_block == 2, pick[2], pick[3])),
        )
        high = jnp.where(lane_block == 0, pick[4], jnp.where(lane_block == 1, pick[5], zero))
        return jnp.concatenate([low, high], axis=1)

    def diagonal(wide):
        tiles = []
        for half in range(2):
            tile = wide[64 * half + 48 : 64 * half + 64, 128 * half : 128 * half + 128]
            for j in range(3):
                start = 64 * half + 16 * j
                tile = jnp.where(
                    lane_block == j, wide[start : start + 16, 128 * half : 128 * half + 128], tile
                )
            tiles.append(tile)
        return tiles

    def coupling(c, carry):
        rows = []
        for u in range(8):
            rows.append(picks_of([pool_rep[codes[f, 8 * c + u]] for f in range(FAR)]))
        rows256 = pl.ds(pl.multiple_of(c * 256, 256), 256)
        blocks = jnp.concatenate([block_s[0, rows256, :], block_s[1, rows256, :]], axis=1).astype(BF)
        tiles = diagonal(dot_nt(jnp.concatenate(rows, axis=0), blocks))
        coupled_s[2 * c] = tiles[0]
        coupled_s[2 * c + 1] = tiles[1]
        return carry

    lax.fori_loop(0, 32, coupling, 0)

    def thirds(t, carry):
        tile = jnp.zeros((16, 128), F32)
        for j in range(4):
            tile = jnp.where(
                lane_block == j, pltpu.roll(upper[4 * t + j, 3].astype(F32), (32 * (j - 2)) % 128, 1), tile
            )
        upper_s[t] = tile.astype(BF)
        return carry

    lax.fori_loop(0, 8, thirds, 0)
    for t in range(4):
        pair = jnp.concatenate([upper_s[2 * t], upper_s[2 * t + 1]], axis=1)
        upper_s[8 + t] = dot(pair, edges_up[512 + 256 * t : 768 + 256 * t, :]).astype(BF)
    for t in range(2):
        pair = jnp.concatenate([upper_s[8 + 2 * t], upper_s[9 + 2 * t]], axis=1)
        upper_s[12 + t] = dot(pair, edges_up[1536 + 256 * t : 1792 + 256 * t, :]).astype(BF)

    def everywhere(tile, block):
        only = jnp.where(lane_block == block, tile, 0.0)
        only = only + pltpu.roll(only, 32, 1)
        return only + pltpu.roll(only, 64, 1)

    rows = []
    for level in range(6):
        node = 512 - (512 >> level) + (device >> level)
        pick = []
        for f in range(FAR):
            q = pup[f, node] - (512 - (512 >> level))
            if level == 0:
                tile, block = upper[q >> 3, (q >> 2) & 1], q & 3
            elif level == 1:
                tile, block = upper[q >> 2, 2], q & 3
            elif level == 2:
                tile, block = upper[q >> 1, 3], q & 1
            elif level == 3:
                tile, block = upper[q, 3], 2
            else:
                tile, block = upper_s[(8 if level == 4 else 12) + (q >> 2)], q & 3
            pick.append(everywhere(tile.astype(F32), block).astype(BF))
        rows.append(picks_of(pick))
    rows += [jnp.zeros((16, 256), BF)] * 2
    tiles = diagonal(dot_nt(jnp.concatenate(rows, axis=0), jnp.concatenate([block_up[0], block_up[1]], axis=1).astype(BF)))
    edge_rows = [me, 8 + (me >> 1), 12 + (me >> 2), 16 + branch, 48 + (branch >> 1)]
    current = everywhere(tiles[1], 1)
    for level in range(4, -1, -1):
        matrix = edges_up[pl.ds(pl.multiple_of(edge_rows[level] * 32, 32), 32), :]
        step = dot_nt(current.astype(BF), jnp.concatenate([matrix] * 4, axis=0))
        current = everywhere(tiles[level // 4], level % 4) + step

    rows6 = first_row(6) * 32
    local_s[63] = coupled_s[63] + dot_nt(current.astype(BF), edges[rows6 : rows6 + 128, :])
    rows5 = first_row(5) * 32
    local_s[62] = coupled_s[62] + dot_nt(local_s[63].astype(BF), edges[rows5 : rows5 + 128, :])
    for level in range(LEVELS - 3, -1, -1):
        parent = first_row(level + 1) // 4
        child = first_row(level) // 4
        for t in range((LEAVES >> level) // 8):
            start = (first_row(level) + 8 * t) * 32
            wide = dot_nt(local_s[parent + t].astype(BF), edges[start : start + 256, :])
            local_s[child + 2 * t] = coupled_s[child + 2 * t] + wide[:, 0:128]
            local_s[child + 2 * t + 1] = coupled_s[child + 2 * t + 1] + wide[:, 128:256]

    sum_s[...] = jnp.zeros((512, 256), F32)

    def back(c, carry):
        lanes = pl.ds(pl.multiple_of(c * 256, 256), 256)
        far = dot(local_s[c].astype(BF), leaf_blocks(basis[:, lanes]))
        parts = []
        for half in range(2):
            first = near_s[4 * c + 2 * half]
            second = near_s[4 * c + 2 * half + 1]
            parts.append(
                jnp.where(left, first + pltpu.roll(first, 64, 1), second + pltpu.roll(second, 64, 1))
            )
        total = (far + INV_FOUR_PI * jnp.concatenate(parts, axis=1)).astype(BF)
        index = order[:, lanes]
        part = index >> 8
        rows = jnp.concatenate(
            [jnp.where(part == low, total, jnp.zeros((16, 256), BF)) for low in range(32)], axis=0
        )
        hot = (iota((256, 256), 0) == (index & 255)).astype(F32).astype(BF)
        sum_s[...] += dot_nt(rows, hot)
        return carry

    lax.fori_loop(0, 32, back, 0)
    for low in range(32):
        out[:, 256 * low : 256 * low + 256] = sum_s[16 * low : 16 * low + 16, :]


def local(order, basis, xyz, table, pool, upper, edges, edges_up, cup, couple, codes, pup, target, source, count):
    return pl.pallas_call(
        local_kernel,
        out_shape=jax.ShapeDtypeStruct((NRHS, POINTS), F32),
        in_specs=[VMEM] * 10 + [SMEM] * 5,
        out_specs=VMEM,
        scratch_shapes=[
            pltpu.VMEM((2 * LEAVES + 2 * HALO, 64, 128), BF),
            pltpu.VMEM((LEAVES, 16, 128), BF),
            pltpu.VMEM((4 * GROUP * TILES, 16, 128), BF),
            pltpu.VMEM((2, 8192, 128), F32),
            pltpu.VMEM((FAR, 16, 1024), F32),
            pltpu.VMEM((2, 256, 128), F32),
            pltpu.VMEM((14, 16, 128), BF),
            pltpu.VMEM((TILES, 16, 128), F32),
            pltpu.VMEM((TILES, 16, 128), F32),
            pltpu.VMEM((LEAVES + 1, 16, 128), F32),
            pltpu.VMEM((512, 256), F32),
        ],
        compiler_params=pltpu.CompilerParams(vmem_limit_bytes=58 * 1024 * 1024),
        name="local",
    )(order, basis, xyz, table, pool, upper, edges, edges_up, cup, couple, codes, pup, target, source, count)


def body(
    right_sides,
    positions,
    point_order,
    leaf_basis,
    transfer,
    couple_local,
    partner_local,
    transfer_up,
    couple_up,
    partner_up,
    send_list,
    side_list,
    pair_target,
    pair_source,
    pair_count,
):
    order = point_order.reshape(1, POINTS)
    starts = jnp.concatenate(
        [jnp.full((LEAVES >> level,), first_row(level), I32) for level in range(LEVELS)]
    )[None, :]
    widths = jnp.concatenate(
        [jnp.full((LEAVES >> level,), LEVELS - level, I32) for level in range(LEVELS)]
    )[None, :]
    partners = partner_local.T
    codes = (partners >> widths) * 256 + starts + (partners & ((1 << widths) - 1))
    codes = jnp.concatenate([codes, jnp.zeros((FAR, 2), I32)], axis=1)
    table, pool, upper, edges, edges_up, cup = exchange(
        right_sides, positions, order, leaf_basis, transfer, transfer_up,
        couple_up.transpose(1, 0, 2), send_list[0], side_list[0],
    )
    return local(
        order, leaf_basis, positions, table, pool.reshape(GROUP * TILES, 16, 128), upper, edges, edges_up, cup,
        couple_local.transpose(1, 0, 2), codes, partner_up.T, pair_target, pair_source, pair_count,
    )


def solution(mesh):
    placed = (
        P(None, ("branch", "row", "top")),
        P(None, ("branch", "row", "top")),
        P(("branch", "row", "top")),
        P(None, ("branch", "row", "top")),
        P(("branch", "row", "top"), None),
        P(("branch", "row", "top"), None, None),
        P(("branch", "row", "top"), None),
        P(),
        P("top", None, None),
        P(),
        P(("branch", "row", "top"), None, None),
        P(("branch", "row", "top"), None, None),
        P(("branch", "row", "top"), None),
        P(("branch", "row", "top"), None),
        P(("branch", "row", "top")),
    )
    return jax.shard_map(
        body,
        mesh=mesh,
        in_specs=placed,
        out_specs=P(None, ("branch", "row", "top")),
        check_vma=False,
    )
```

profile of v0, /device:TPU:15, one launch (start us, length us, event | category | flops | bytes accessed | tf_op | source)
XLA Modules:
  0.0 163.2 jit_solution(16834145503372521239)
XLA Ops:
  0.7 0.7 add_bitcast_fusion
  1.4 0.6 concatenate.3.codes
  2.0 0.0 copy-start
  2.0 1.0 copy-done
  3.0 0.0 copy-start.2
  3.0 1.2 copy-done.2
  4.2 0.0 copy-start.5
  4.3 1.0 copy-done.5
  5.3 0.0 copy-start.6
  5.3 0.8 copy-done.6
  6.1 0.0 copy-start.7
  6.1 0.9 copy-done.7
  7.1 0.0 copy-start.9
  7.1 0.8 copy-done.9
  7.8 0.0 copy-start.10
  7.8 0.7 copy-done.10
  8.5 0.0 copy-start.11
  8.5 0.7 copy-done.11
  9.2 58.0 %exchange.1 = (bf16[320,16,128]{2,1,0:T(8,128)(2,1)S(1)}, bf16[8,64,16,128]{3,2,1,0:T(8,128)(2,1)}, bf16[32,4,16,128]{3,2,1,0:T(8,128)(2,1)S(1)}, bf16[8192,128]...) custom-call(bf16[16,8192]{1,0:T(8,128)(2,1)S(1)} %copy-done.7, ...), custom_call_target="tpu_custom_call" | custom-call | tf_op jit(solution)/shard_map/exchange/pallas_call | solution.py:359
  67.3 0.0 copy-start.1
  67.3 1.1 copy-done.1
  68.4 0.0 copy-start.3
  68.4 0.8 copy-done.3
  69.2 0.0 copy-start.4
  69.2 0.8 copy-done.4
  70.0 0.0 copy-start.8
  70.0 0.7 copy-done.8
  70.7 92.5 %local.1 = f32[16,8192]{1,0:T(8,128)} custom-call(s32[1,8192]{1,0:T(1,128)} %bitcast.9, bf16[32,8192]{1,0:T(8,128)(2,1)} %basis.3, bf16[3,8192]{1,0:T(4,128)(2,1)} %xyz.3, bf16[320,16,128]{2,1,0:T(8,128)(2,1)} %copy-done.1, bf16[512,16,128]{2,1,0:T(8,128)(2,1)} %bitcast.15, bf16[32,4,16,128]{3,2,1,0:T(8,128)(2,1)} %copy-done.3, ...), custom_call_target="tpu_custom_call" | custom-call | tf_op jit(solution)/shard_map/local/pallas_call | solution.py:645
Async XLA Ops:
  2.0 1.0 copy-start
  3.0 1.2 copy-start.2
  4.2 1.0 copy-start.5
  5.3 0.8 copy-start.6
  6.1 0.9 copy-start.7
  7.1 0.8 copy-start.9
  7.8 0.7 copy-start.10
  8.5 0.7 copy-start.11
  67.3 1.1 copy-start.1
  68.4 0.8 copy-start.3
  69.2 0.8 copy-start.4
  70.0 0.7 copy-start.8
where the time goes:
time: 164 us; the launch traced here: 163 us
  Pallas kernels  151 us (92%)
  local copies, waits for them, and re-layouts  11.2 us (7%)
    pallas_call x1, Pallas kernels, local(): pl.pallas_call(local_kernel, out_shape=jax.ShapeDtypeStruct((NRHS, POINTS...  92.5 us
    pallas_call x1, Pallas kernels, exchange(): pl.pallas_call(exchange_kernel, out_shape=(shape((2 * LEAVES + 2 * HALO,...  58 us
    unnamed x24, local copies, waits for them, and re-layouts  10.6 us

commit v1 on v0

v1 whole, which is shorter than its diff:
```python
import jax
import jax.numpy as jnp
from jax import lax
from jax.experimental import pallas as pl
from jax.experimental.pallas import tpu as pltpu
from jax.sharding import PartitionSpec as P

LEAF = 64
RANK = 32
NRHS = 16
FAR = 6
SLOT = 16
HALO = 32
LEAVES = 128
POINTS = LEAVES * LEAF
NODES = 2 * LEAVES - 2
GROUP = 8
BRANCHES = 32
UPPER = 504
LEVELS = 7
TILES = 64

INV_FOUR_PI = 0.07957747154594767
SOFTENING = 0.01

BF = jnp.bfloat16
F32 = jnp.float32
I32 = jnp.int32
MESH = pl.DeviceIdType.MESH
VMEM = pl.BlockSpec(memory_space=pltpu.VMEM)
SMEM = pl.BlockSpec(memory_space=pltpu.SMEM)
HBM = pl.BlockSpec(memory_space=pltpu.HBM)


def dot(a, b):
    return jnp.dot(a, b, preferred_element_type=F32)


def dot_nt(a, b):
    return lax.dot_general(a, b, (((1,), (1,)), ((), ())), preferred_element_type=F32)


def iota(shape, axis):
    return lax.broadcasted_iota(I32, shape, axis)


def first_row(level):
    return 2 * LEAVES - 2 * (LEAVES >> level)


def block_turns(value):
    return [value] + [pltpu.roll(value, 32 * step, 1) for step in range(1, 4)]


def spread_edges(rows_of, put):
    value = rows_of(0)
    shape = value.shape
    owner = (iota(shape, 0) >> 1) & 3
    lane = iota(shape, 1) >> 5
    masks = [(owner == k) & (lane == k) for k in range(4)]
    for g in range(8):
        turns = block_turns(rows_of(g))
        for p in range(4):
            out = jnp.zeros(shape, F32)
            for k in range(4):
                out = jnp.where(masks[k], turns[(k - p) % 4], out)
            put(4 * g + p, out)


def spread_blocks(rows_of, put):
    lane = None
    for g in range(8):
        turns = [block_turns(rows_of(f, g)) for f in range(FAR)]
        if lane is None:
            lane = iota(turns[0][0].shape, 1) >> 5
        for a in range(4):
            pick = [turns[f][(f % 4 - a) % 4] for f in range(FAR)]
            low = jnp.where(
                lane == 0, pick[0], jnp.where(lane == 1, pick[1], jnp.where(lane == 2, pick[2], pick[3]))
            )
            high = jnp.where(lane == 0, pick[4], jnp.where(lane == 1, pick[5], 0.0))
            put(4 * g + a, low, high)


def stack_rows(rows, shape):
    sub = iota(shape, 0)
    out = jnp.zeros(shape, F32)
    for k, row in enumerate(rows):
        out = jnp.where(sub == k, row, out)
    return out


def split_three(value):
    high = value.astype(BF).astype(F32)
    rest = value - high
    middle = rest.astype(BF).astype(F32)
    return high, middle, rest - middle


def source_features(xyz):
    x, y, z = xyz[0:1], xyz[1:2], xyz[2:3]
    high, middle, low = split_three(x * x + y * y + z * z)
    return stack_rows([x, y, z, 1.0, 1.0, 1.0, high, middle, low], (16, xyz.shape[1]))


def target_features(xyz):
    x, y, z = xyz[0:1], xyz[1:2], xyz[2:3]
    high, middle, low = split_three(x * x + y * y + z * z + SOFTENING)
    return stack_rows(
        [-2.0 * x, -2.0 * y, -2.0 * z, high, middle, low, 1.0, 1.0, 1.0], (16, xyz.shape[1])
    )


def leaf_blocks(basis):
    lane = iota(basis.shape, 1) >> 6
    zero = jnp.zeros(basis.shape, basis.dtype)
    return jnp.concatenate([jnp.where(lane == j, basis, zero) for j in range(4)], axis=0)


def exchange_kernel(
    rhs_h, xyz_h, order_h, basis_h, trans_h, tup_h, cup_h, couple_h, partner_h, send_h, side_h,
    table_o, pool_o, upper_o, edges_o, edges_up_o, cup_o, blocks_o, codes_o,
    rhs, xyz, order, basis, trans, tup, cup, couple, partner, send_s, side_s,
    x_s, table_s, pool_s, edge_s, tail_s, near_s, side_buf, root_s, roots_s, upper_s, cup_own, cup_send, cup_recv,
    edges, edges_up, block_s, block_tail, blocks, codes,
    in_sem, near_send, near_recv, core_send, core_recv, ring_send, ring_recv,
    root_send, root_recv, up_send, up_recv, cup_sem, local_sem,
):
    branch = lax.axis_index("branch")
    row = lax.axis_index("row")
    top = lax.axis_index("top")
    me = row * 2 + top
    device = branch * GROUP + me

    held = (rhs, xyz, order, basis, trans, tup, cup, couple, partner, send_s, side_s)
    given = (rhs_h, xyz_h, order_h, basis_h, trans_h, tup_h, cup_h, couple_h, partner_h, send_h, side_h)
    fetched = [pltpu.make_async_copy(a, b, in_sem.at[i]) for i, (a, b) in enumerate(zip(given, held))]
    for i in (0, 2, 1, 3, 9, 10, 4, 5, 6, 7, 8):
        fetched[i].start()

    def member(index):
        return (branch, index // 2, index % 2)

    def peer(offset):
        return (me + offset) % GROUP

    def cousin(offset):
        return ((branch + offset) % BRANCHES, row, top)

    barrier = pltpu.get_barrier_semaphore()
    for offset in range(1, GROUP):
        pl.semaphore_signal(barrier, inc=1, device_id=member(peer(offset)), device_id_type=MESH)

    def greet(offset, carry):
        pl.semaphore_signal(barrier, inc=1, device_id=cousin(offset), device_id_type=MESH)
        return carry

    lax.fori_loop(1, BRANCHES, greet, 0)

    for i in range(4):
        fetched[i].wait()
    for low in range(32):
        x_s[16 * low : 16 * low + 16, :] = rhs[:, 256 * low : 256 * low + 256]
    row_id = iota((256, 256), 0).astype(F32).astype(BF)
    left = iota((16, 128), 1) < 64

    def chunk(c, carry):
        lanes = pl.ds(pl.multiple_of(c * 512, 512), 512)
        index = order[:, lanes]
        fine = jnp.broadcast_to((index & 255).astype(F32), (16, 512)).astype(BF)
        hots = []
        for k in range(2):
            column = jnp.concatenate([fine[:, 256 * k : 256 * k + 256]] * 16, axis=0)
            hots.append(jnp.where(row_id == column, jnp.ones((), BF), jnp.zeros((), BF)))
        wide = dot(x_s[...], jnp.concatenate(hots, axis=1))
        part = jnp.broadcast_to(index >> 8, (16, 512))
        ordered = jnp.zeros((16, 512), F32)
        for low in range(32):
            ordered = jnp.where(part == low, wide[16 * low : 16 * low + 16], ordered)
        features = source_features(xyz[:, lanes].astype(F32))
        for half in range(4):
            value = ordered[:, 128 * half : 128 * half + 128]
            extra = features[:, 128 * half : 128 * half + 128]
            table_s[8 * c + 2 * half] = jnp.where(left, value, pltpu.roll(extra, 64, 1)).astype(BF)
            table_s[8 * c + 2 * half + 1] = jnp.where(left, pltpu.roll(value, 64, 1), extra).astype(BF)
        rounded = ordered.astype(BF)
        columns = basis[:, lanes]
        for k in range(2):
            pool_s[2 * c + k] = dot_nt(
                rounded[:, 256 * k : 256 * k + 256], leaf_blocks(columns[:, 256 * k : 256 * k + 256])
            ).astype(BF)
        return carry

    lax.fori_loop(0, 16, chunk, 0, unroll=2)

    fetched[9].wait()
    fetched[10].wait()

    def fill(k, carry):
        for m in range(GROUP):
            near_s[m, k] = table_s[send_s[m, k]]
        for s in range(2):
            side_buf[s, 2 * k] = table_s[side_s[s, 2 * k]]
            side_buf[s, 2 * k + 1] = table_s[side_s[s, 2 * k + 1]]
        return carry

    lax.fori_loop(0, SLOT, fill, 0)

    pl.semaphore_wait(barrier, GROUP - 1 + BRANCHES - 1)

    sent = []

    def send(src, dst, send_sem, recv_sem, device_id):
        copy = pltpu.make_async_remote_copy(
            src_ref=src, dst_ref=dst, send_sem=send_sem, recv_sem=recv_sem,
            device_id=device_id, device_id_type=MESH,
        )
        copy.start()
        sent.append(copy)
        return copy

    kept = []

    def keep(src, dst, sem):
        copy = pltpu.make_async_copy(src, dst, sem)
        copy.start()
        kept.append(copy)

    partner_core = (branch, row, 1 - top)
    next_row = (branch, (row + 1) % 4, top)
    last_row = (branch, (row + 3) % 4, top)
    before = ((row + 3) % 4) * 2 + top
    after = ((row + 1) % 4) * 2 + top
    across = ((row + 2) % 4) * 2 + top

    def ring_first(p, src):
        tiles = pl.ds(32 * p, 32)
        one = send(src, pool_o.at[me, tiles], ring_send.at[4 * p], ring_recv.at[4 * p], next_row)
        two = send(src, pool_o.at[me, tiles], ring_send.at[4 * p + 1], ring_recv.at[4 * p + 1], last_row)
        core = send(src, pool_o.at[me, tiles], core_send.at[5 * p], core_recv.at[5 * p], partner_core)
        return one, two, core

    def ring_second(p, first):
        tiles = pl.ds(32 * p, 32)
        first[0].wait_recv()
        lower = pl.ds(32 * p, 16)
        three = send(
            pool_o.at[before, lower], pool_o.at[before, lower],
            ring_send.at[4 * p + 2], ring_recv.at[4 * p + 2], next_row,
        )
        a = send(
            pool_o.at[before, tiles], pool_o.at[before, tiles],
            core_send.at[5 * p + 1], core_recv.at[5 * p + 1], partner_core,
        )
        first[1].wait_recv()
        higher = pl.ds(32 * p + 16, 16)
        four = send(
            pool_o.at[after, higher], pool_o.at[after, higher],
            ring_send.at[4 * p + 3], ring_recv.at[4 * p + 3], last_row,
        )
        b = send(
            pool_o.at[after, tiles], pool_o.at[after, tiles],
            core_send.at[5 * p + 2], core_recv.at[5 * p + 2], partner_core,
        )
        return three, four, a, b

    def ring_third(p, second):
        second[0].wait_recv()
        lower = pl.ds(32 * p, 16)
        a = send(
            pool_o.at[across, lower], pool_o.at[across, lower],
            core_send.at[5 * p + 3], core_recv.at[5 * p + 3], partner_core,
        )
        second[1].wait_recv()
        higher = pl.ds(32 * p + 16, 16)
        b = send(
            pool_o.at[across, higher], pool_o.at[across, higher],
            core_send.at[5 * p + 4], core_recv.at[5 * p + 4], partner_core,
        )
        return a, b

    leaves_first = ring_first(0, pool_s.at[pl.ds(0, 32)])
    arriving = [leaves_first[2]]
    for offset in range(1, GROUP):
        arriving.append(
            send(
                near_s.at[peer(offset)], table_o.at[pl.ds(LEAVES + me * SLOT, SLOT)],
                near_send.at[offset - 1], near_recv.at[offset - 1], member(peer(offset)),
            )
        )
    arriving.append(
        send(
            side_buf.at[1], table_o.at[pl.ds(2 * LEAVES, HALO)],
            near_send.at[7], near_recv.at[7], cousin(1),
        )
    )
    arriving.append(
        send(
            side_buf.at[0], table_o.at[pl.ds(2 * LEAVES + HALO, HALO)],
            near_send.at[8], near_recv.at[8], cousin(BRANCHES - 1),
        )
    )
    keep(table_s, table_o.at[pl.ds(0, LEAVES)], local_sem.at[0])
    keep(near_s.at[me], table_o.at[pl.ds(LEAVES + me * SLOT, SLOT)], local_sem.at[1])

    fetched[4].wait()
    tail_s[...] = jnp.zeros((16, 1024), F32)
    tail_s[0:14, :] = trans[240:254, :].astype(F32)

    def spread_one(rows_of, start, part):
        def put(p, out):
            edge_s[part, pl.ds(p, 16, stride=32), :] = out

        spread_edges(rows_of, put)
        edges[pl.ds(start, 512), :] = edge_s[part, 0:512].astype(BF)

    def spread(c, carry):
        for part in range(3):
            start = pl.multiple_of(48 * c + 16 * part, 16)
            spread_one(
                lambda g: trans[pl.ds(start, 16), 128 * g : 128 * g + 128].astype(F32),
                pl.multiple_of(1536 * c + 512 * part, 512), part,
            )
        return carry

    lax.fori_loop(0, 5, spread, 0)
    spread_one(lambda g: tail_s[:, 128 * g : 128 * g + 128], 7680, 0)
    keep(edges, edges_o, local_sem.at[4])

    tile_of = [first_row(level) // 4 for level in range(LEVELS)]
    for level in range(LEVELS - 2):
        for t in range((LEAVES >> level) // 8):
            child = tile_of[level] + 2 * t
            pair = jnp.concatenate([pool_s[child], pool_s[child + 1]], axis=1)
            rows = (first_row(level) + 8 * t) * 32
            pool_s[tile_of[level + 1] + t] = dot(pair, edges[rows : rows + 256, :]).astype(BF)
    rows = first_row(5) * 32
    pool_s[63] = dot(pool_s[62], edges[rows : rows + 128, :]).astype(BF)
    rows = first_row(6) * 32
    root = dot(pool_s[63], edges[rows : rows + 128, :])
    placed = root
    for k in (0, 1, 3):
        placed = jnp.where(me % 4 == k, pltpu.roll(root, (32 * (k - 2)) % 128, 1), placed)
    root_s[...] = placed.astype(BF)
    roots = []
    for offset in range(1, GROUP):
        roots.append(
            send(
                root_s, roots_s.at[me],
                root_send.at[offset - 1], root_recv.at[offset - 1], member(peer(offset)),
            )
        )
    roots_s[me] = root_s[...]
    rest_first = ring_first(1, pool_s.at[pl.ds(32, 32)])
    arriving.append(rest_first[2])
    keep(pool_s, pool_o.at[me], local_sem.at[2])
    leaves_second = ring_second(0, leaves_first)
    arriving += leaves_second[2:]

    fetched[5].wait()
    slot = iota((64, 496), 0)
    want = jnp.where(
        slot < 8,
        8 * branch + slot,
        jnp.where(
            slot < 12,
            248 + 4 * branch + slot,
            jnp.where(slot < 14, 372 + 2 * branch + slot, jnp.where(slot < 16, -1, 432 + slot)),
        ),
    )
    chosen = dot((iota((64, 496), 1) == want).astype(F32).astype(BF), tup[...])

    def put_up(p, out):
        edge_s[0, pl.ds(p, 64, stride=32), :] = out

    spread_edges(lambda g: chosen[:, 128 * g : 128 * g + 128], put_up)
    edges_up[...] = edge_s[0].astype(BF)
    keep(edges_up, edges_up_o, local_sem.at[5])

    for copy in roots:
        copy.wait_recv()
    low = roots_s[0] + roots_s[1] + roots_s[2] + roots_s[3]
    high = roots_s[4] + roots_s[5] + roots_s[6] + roots_s[7]
    upper_s[0] = low
    upper_s[1] = high
    first = dot(jnp.concatenate([low, high], axis=1), edges_up[0:256, :]).astype(BF)
    upper_s[2] = first
    second = dot(first, edges_up[256:384, :]).astype(BF)
    third = dot(second[:, 0:64], edges_up[384:448, :]).astype(BF)
    upper_s[3] = jnp.where(iota((16, 128), 1) < 64, second.astype(F32), third.astype(F32)).astype(BF)

    def spread_up(offset, carry):
        pltpu.make_async_remote_copy(
            src_ref=upper_s, dst_ref=upper_o.at[branch],
            send_sem=up_send.at[offset - 1], recv_sem=up_recv.at[offset - 1],
            device_id=cousin(offset), device_id_type=MESH,
        ).start()
        return carry

    lax.fori_loop(1, BRANCHES, spread_up, 0)
    keep(upper_s, upper_o.at[branch], local_sem.at[3])

    fetched[6].wait()
    slot = iota((16, 252), 0)
    shape = slot & 7
    base = jnp.where(slot < 8, device, device + 1 - 2 * top)
    node = jnp.full((16, 252), -1, I32)
    for level in range(6):
        node = jnp.where(shape == level, 512 - (512 >> level) + (base >> level), node)
    hot = (iota((16, 252), 1) + 252 * top == node).astype(F32).astype(BF)
    for f in range(FAR):
        chosen = dot(hot, cup[f])
        cup_own[f] = chosen[0:8]
        cup_send[f] = chosen[8:16]
    cup_copy = send(cup_send, cup_recv, cup_sem.at[0], cup_sem.at[1], partner_core)

    fetched[8].wait()
    column = iota((FAR, 254), 1)
    width = jnp.full((FAR, 254), 7, I32)
    start = jnp.zeros((FAR, 254), I32)
    for level in range(1, LEVELS):
        width = jnp.where(column >= first_row(level), 7 - level, width)
        start = jnp.where(column >= first_row(level), first_row(level), start)
    codes[:, 254:256] = jnp.zeros((FAR, 2), I32)
    codes[:, 0:254] = (partner[...] >> width) * 256 + start + (partner[...] & ((1 << width) - 1))
    keep(codes, codes_o, local_sem.at[6])

    fetched[7].wait()
    for f in range(FAR):
        block_tail[f] = jnp.zeros((16, 1024), F32)
        block_tail[f, 0:14, :] = couple[f, 240:254, :].astype(F32)

    def couple_one(rows_of, start, part):
        def put(a, low, high):
            block_s[part, 0, pl.ds(a, 16, stride=32), :] = low
            block_s[part, 1, pl.ds(a, 16, stride=32), :] = high

        spread_blocks(rows_of, put)
        blocks[pl.ds(start, 512), 0:128] = block_s[part, 0].astype(BF)
        blocks[pl.ds(start, 512), 128:256] = block_s[part, 1].astype(BF)

    def couple_rows(c, carry):
        start = pl.multiple_of(16 * c, 16)
        couple_one(
            lambda f, g: couple[f, pl.ds(start, 16), 128 * g : 128 * g + 128].astype(F32),
            pl.multiple_of(512 * c, 512), 0,
        )
        return carry

    lax.fori_loop(0, 8, couple_rows, 0)
    rest_second = ring_second(1, rest_first)
    arriving += rest_second[2:]
    arriving += ring_third(0, leaves_second)
    lax.fori_loop(8, 15, couple_rows, 0)
    arriving += ring_third(1, rest_second)
    couple_one(lambda f, g: block_tail[f, :, 128 * g : 128 * g + 128], 7680, 0)
    keep(blocks, blocks_o, local_sem.at[7])

    cup_copy.wait_recv()
    cup_own[...] = cup_own[...] + cup_recv[...]
    keep(cup_own, cup_o, local_sem.at[8])
    for copy in arriving:
        copy.wait_recv()
    for copy in sent:
        copy.wait_send()

    def finish(offset, carry):
        pltpu.make_async_remote_copy(
            src_ref=upper_s, dst_ref=upper_o.at[branch],
            send_sem=up_send.at[offset - 1], recv_sem=up_recv.at[offset - 1],
            device_id=cousin(offset), device_id_type=MESH,
        ).wait()
        return carry

    lax.fori_loop(1, BRANCHES, finish, 0)
    for copy in kept:
        copy.wait()


def exchange(rhs, xyz, order, basis, trans, tup, cup, couple, partner, send_list, side_list):
    shape = jax.ShapeDtypeStruct
    inputs = (rhs, xyz, order, basis, trans, tup, cup, couple, partner, send_list, side_list)
    return pl.pallas_call(
        exchange_kernel,
        out_shape=(
            shape((2 * LEAVES + 2 * HALO, 16, 128), BF),
            shape((GROUP, TILES, 16, 128), BF),
            shape((BRANCHES, 4, 16, 128), BF),
            shape((8192, 128), BF),
            shape((2048, 128), BF),
            shape((FAR, 8, 1024), F32),
            shape((8192, 256), BF),
            shape((FAR, 256), I32),
        ),
        in_specs=[HBM] * 11,
        out_specs=(HBM,) * 8,
        scratch_shapes=[pltpu.VMEM(value.shape, value.dtype) for value in inputs[:9]]
        + [pltpu.SMEM(value.shape, value.dtype) for value in inputs[9:]]
        + [
            pltpu.VMEM((512, 256), BF),
            pltpu.VMEM((LEAVES, 16, 128), BF),
            pltpu.VMEM((TILES, 16, 128), BF),
            pltpu.VMEM((3, 2048, 128), F32),
            pltpu.VMEM((16, 1024), F32),
            pltpu.VMEM((GROUP, SLOT, 16, 128), BF),
            pltpu.VMEM((2, HALO, 16, 128), BF),
            pltpu.VMEM((16, 128), BF),
            pltpu.VMEM((GROUP, 16, 128), BF),
            pltpu.VMEM((4, 16, 128), BF),
            pltpu.VMEM((FAR, 8, 1024), F32),
            pltpu.VMEM((FAR, 8, 1024), F32),
            pltpu.VMEM((FAR, 8, 1024), F32),
            pltpu.VMEM((8192, 128), BF),
            pltpu.VMEM((2048, 128), BF),
            pltpu.VMEM((1, 2, 512, 128), F32),
            pltpu.VMEM((FAR, 16, 1024), F32),
            pltpu.VMEM((8192, 256), BF),
            pltpu.VMEM((FAR, 256), I32),
        ]
        + [
            pltpu.SemaphoreType.DMA((count,))
            for count in (11, 9, 9, 10, 10, 8, 8, 7, 7, BRANCHES - 1, BRANCHES - 1, 2, 9)
        ],
        compiler_params=pltpu.CompilerParams(
            collective_id=0, has_side_effects=True, vmem_limit_bytes=48 * 1024 * 1024
        ),
        name="exchange",
    )(*inputs)


def local_kernel(
    table_h, target_h, source_h, count_h, xyz_h, pool_h, blocks_h, codes_h, upper_h, edges_up_h, cup_h, pup_h,
    edges_h, basis_h, order_h,
    out,
    table, target, source, count, xyz, pool, blocks, codes, upper, edges_up, cup, pup, edges, basis, order,
    swap_s, goal_s, pool_rep, block_up, upper_s, coupled_s, local_s, near_s, sum_s, in_sem,
):
    given = (table_h, target_h, source_h, count_h, xyz_h, pool_h, blocks_h, codes_h, upper_h, edges_up_h, cup_h, pup_h,
             edges_h, basis_h, order_h)
    held = (table, target, source, count, xyz, pool, blocks, codes, upper, edges_up, cup, pup, edges, basis, order)
    fetched = [pltpu.make_async_copy(a, b, in_sem.at[i]) for i, (a, b) in enumerate(zip(given, held))]
    for copy in fetched:
        copy.start()
    for copy in fetched[:5]:
        copy.wait()
    branch = lax.axis_index("branch")
    me = lax.axis_index("row") * 2 + lax.axis_index("top")
    device = branch * GROUP + me
    left = iota((16, 128), 1) < 64
    lane_block = iota((16, 128), 1) >> 5

    eye = (iota((128, 128), 0) == iota((128, 128), 1)).astype(F32).astype(BF)

    def goals(c, carry):
        lanes = pl.ds(pl.multiple_of(c * 128, 128), 128)
        features = target_features(xyz[:, lanes].astype(F32)).astype(BF)
        turned = dot_nt(eye, jnp.concatenate([features] * 4, axis=0)).astype(BF)
        goal_s[2 * c] = turned[0:64]
        goal_s[2 * c + 1] = turned[64:128]
        return carry

    lax.fori_loop(0, 64, goals, 0, unroll=16)

    def swaps(c, carry):
        tiles = table[pl.ds(8 * c, 8)].reshape(128, 128).astype(F32)
        swap_s[pl.ds(8 * c, 8)] = pltpu.roll(tiles, 64, 1).astype(BF).reshape(8, 16, 128)
        return carry

    lax.fori_loop(0, 40, swaps, 0, unroll=4)

    def clear(t, carry):
        near_s[t] = jnp.zeros((16, 64), F32)
        return carry

    lax.fori_loop(0, LEAVES + 1, clear, 0, unroll=3)

    live = count[0]
    lane16 = (iota((64, 64), 1) >> 4)
    zero = jnp.zeros((16, 128), BF)

    def quad(first):
        at = [source[0, first + i] for i in range(4)]
        to = [target[0, first + i] for i in range(4)]
        g = [goal_s[to[i]] for i in range(4)]
        lhs = jnp.where(lane16 == 0, g[0], jnp.where(lane16 == 1, g[1], jnp.where(lane16 == 2, g[2], g[3])))
        value, other = [], []
        for i in range(4):
            plain, swapped = table[at[i]], swap_s[at[i]]
            if i % 2 == 0:
                pieces = [jnp.where(left, plain, zero), jnp.where(left, swapped, zero)]
            else:
                pieces = [jnp.where(left, zero, swapped), jnp.where(left, zero, plain)]
            for rows, piece in zip((value, other), pieces):
                rows.append(jnp.concatenate([piece, zero] if i < 2 else [zero, piece], axis=1))
        tile = lax.rsqrt(dot(lhs, jnp.concatenate(other, axis=0))).astype(BF)
        wide = dot_nt(jnp.concatenate(value, axis=0), tile)
        return [
            (jnp.where(first + i < live, to[i], LEAVES), wide[16 * i : 16 * i + 16]) for i in range(4)
        ]

    def near(c, carry):
        outs = []
        for k in range(16):
            outs += quad(c * 64 + 4 * k)
        for goal, part in outs:
            near_s[goal] = near_s[goal] + part
        return carry

    lax.fori_loop(0, (live + 63) // 64, near, 0)

    for copy in fetched[5:12]:
        copy.wait()

    def put_up(a, low, high):
        block_up[0, pl.ds(a, 8, stride=32), :] = low
        block_up[1, pl.ds(a, 8, stride=32), :] = high

    spread_blocks(lambda f, g: cup[f, :, 128 * g : 128 * g + 128], put_up)

    wide_block = iota((128, 128), 1) >> 5

    def widen(t, carry):
        tiles = pool[pl.ds(8 * t, 8)].reshape(128, 128).astype(F32)
        turns = [v.astype(BF) for v in block_turns(tiles)]
        for j in range(4):
            value = turns[(3 - j) % 4]
            for k in range(3):
                value = jnp.where(wide_block == k, turns[(k - j) % 4], value)
            pool_rep[pl.ds(8 * t, 8), j] = value.reshape(8, 16, 128)
        return carry

    lax.fori_loop(0, GROUP * TILES // 8, widen, 0, unroll=4)

    def picks_of(pick):
        low = jnp.where(
            lane_block == 0,
            pick[0],
            jnp.where(lane_block == 1, pick[1], jnp.where(lane_block == 2, pick[2], pick[3])),
        )
        high = jnp.where(lane_block == 0, pick[4], jnp.where(lane_block == 1, pick[5], zero))
        return jnp.concatenate([low, high], axis=1)

    def diagonal(wide):
        tiles = []
        for half in range(2):
            tile = wide[64 * half + 48 : 64 * half + 64, 128 * half : 128 * half + 128]
            for j in range(3):
                start = 64 * half + 16 * j
                tile = jnp.where(
                    lane_block == j, wide[start : start + 16, 128 * half : 128 * half + 128], tile
                )
            tiles.append(tile)
        return tiles

    def coupling(c, carry):
        rows = []
        for u in range(8):
            rows.append(picks_of([pool_rep[codes[f, 8 * c + u] >> 2, codes[f, 8 * c + u] & 3] for f in range(FAR)]))
        matrices = blocks[pl.ds(pl.multiple_of(c * 256, 256), 256), :]
        tiles = diagonal(dot_nt(jnp.concatenate(rows, axis=0), matrices))
        coupled_s[2 * c] = tiles[0]
        coupled_s[2 * c + 1] = tiles[1]
        return carry

    lax.fori_loop(0, 32, coupling, 0, unroll=4)

    def thirds(t, carry):
        tile = jnp.zeros((16, 128), F32)
        for j in range(4):
            tile = jnp.where(
                lane_block == j, pltpu.roll(upper[4 * t + j, 3].astype(F32), (32 * (j - 2)) % 128, 1), tile
            )
        upper_s[t] = tile.astype(BF)
        return carry

    lax.fori_loop(0, 8, thirds, 0)
    for t in range(4):
        pair = jnp.concatenate([upper_s[2 * t], upper_s[2 * t + 1]], axis=1)
        upper_s[8 + t] = dot(pair, edges_up[512 + 256 * t : 768 + 256 * t, :]).astype(BF)
    for t in range(2):
        pair = jnp.concatenate([upper_s[8 + 2 * t], upper_s[9 + 2 * t]], axis=1)
        upper_s[12 + t] = dot(pair, edges_up[1536 + 256 * t : 1792 + 256 * t, :]).astype(BF)

    def everywhere(tile, block):
        only = jnp.where(lane_block == block, tile, 0.0)
        only = only + pltpu.roll(only, 32, 1)
        return only + pltpu.roll(only, 64, 1)

    rows = []
    for level in range(6):
        node = 512 - (512 >> level) + (device >> level)
        pick = []
        for f in range(FAR):
            q = pup[f, node] - (512 - (512 >> level))
            if level == 0:
                tile, block = upper[q >> 3, (q >> 2) & 1], q & 3
            elif level == 1:
                tile, block = upper[q >> 2, 2], q & 3
            elif level == 2:
                tile, block = upper[q >> 1, 3], q & 1
            elif level == 3:
                tile, block = upper[q, 3], 2
            else:
                tile, block = upper_s[(8 if level == 4 else 12) + (q >> 2)], q & 3
            pick.append(everywhere(tile.astype(F32), block).astype(BF))
        rows.append(picks_of(pick))
    rows += [jnp.zeros((16, 256), BF)] * 2
    tiles = diagonal(dot_nt(jnp.concatenate(rows, axis=0), jnp.concatenate([block_up[0], block_up[1]], axis=1).astype(BF)))
    edge_rows = [me, 8 + (me >> 1), 12 + (me >> 2), 16 + branch, 48 + (branch >> 1)]
    current = everywhere(tiles[1], 1)
    for level in range(4, -1, -1):
        matrix = edges_up[pl.ds(pl.multiple_of(edge_rows[level] * 32, 32), 32), :]
        step = dot_nt(current.astype(BF), jnp.concatenate([matrix] * 4, axis=0))
        current = everywhere(tiles[level // 4], level % 4) + step

    for copy in fetched[12:]:
        copy.wait()
    rows6 = first_row(6) * 32
    local_s[63] = coupled_s[63] + dot_nt(current.astype(BF), edges[rows6 : rows6 + 128, :])
    rows5 = first_row(5) * 32
    local_s[62] = coupled_s[62] + dot_nt(local_s[63].astype(BF), edges[rows5 : rows5 + 128, :])
    for level in range(LEVELS - 3, -1, -1):
        parent = first_row(level + 1) // 4
        child = first_row(level) // 4
        for t in range((LEAVES >> level) // 8):
            start = (first_row(level) + 8 * t) * 32
            wide = dot_nt(local_s[parent + t].astype(BF), edges[start : start + 256, :])
            local_s[child + 2 * t] = coupled_s[child + 2 * t] + wide[:, 0:128]
            local_s[child + 2 * t + 1] = coupled_s[child + 2 * t + 1] + wide[:, 128:256]

    sum_s[...] = jnp.zeros((512, 256), F32)

    def back(c, carry):
        tall, hots = [], []
        lows = []
        for k in range(4):
            lanes = pl.ds(pl.multiple_of((4 * c + k) * 256, 256), 256)
            far = dot(local_s[4 * c + k].astype(BF), leaf_blocks(basis[:, lanes]))
            parts = []
            for half in range(2):
                first = near_s[16 * c + 4 * k + 2 * half]
                second = near_s[16 * c + 4 * k + 2 * half + 1]
                parts += [first, second]
            tall.append((far + INV_FOUR_PI * jnp.concatenate(parts, axis=1)).astype(BF))
            index = order[:, lanes]
            lows.append(jnp.broadcast_to((index >> 8).astype(F32), (16, 256)).astype(BF))
            fine = jnp.broadcast_to((index & 255).astype(F32), (16, 256)).astype(BF)
            fine = jnp.concatenate([fine] * 16, axis=0)
            hots.append(jnp.where(row_id == fine, jnp.ones((), BF), jnp.zeros((), BF)))
        total = jnp.concatenate(tall, axis=1)
        part = jnp.concatenate(lows, axis=1)
        none = jnp.zeros((16, 1024), BF)
        rows = jnp.concatenate(
            [jnp.where(part == jnp.asarray(low, BF), total, none) for low in range(32)], axis=0
        )
        sum_s[...] += dot_nt(rows, jnp.concatenate(hots, axis=1))
        return carry

    row_id = iota((256, 256), 0).astype(F32).astype(BF)
    lax.fori_loop(0, 8, back, 0)
    for low in range(32):
        out[:, 256 * low : 256 * low + 256] = sum_s[16 * low : 16 * low + 16, :]


def local(table, target, source, count, xyz, pool, blocks, codes, upper, edges_up, cup, pup, edges, basis, order):
    inputs = (table, target, source, count, xyz, pool, blocks, codes, upper, edges_up, cup, pup, edges, basis, order)
    scalars = (1, 2, 3, 7, 11)
    return pl.pallas_call(
        local_kernel,
        out_shape=jax.ShapeDtypeStruct((NRHS, POINTS), F32),
        in_specs=[HBM] * 15,
        out_specs=VMEM,
        scratch_shapes=[
            (pltpu.SMEM if i in scalars else pltpu.VMEM)(value.shape, value.dtype) for i, value in enumerate(inputs)
        ]
        + [
            pltpu.VMEM((2 * LEAVES + 2 * HALO, 16, 128), BF),
            pltpu.VMEM((LEAVES, 64, 64), BF),
            pltpu.VMEM((GROUP * TILES, 4, 16, 128), BF),
            pltpu.VMEM((2, 256, 128), F32),
            pltpu.VMEM((14, 16, 128), BF),
            pltpu.VMEM((TILES, 16, 128), F32),
            pltpu.VMEM((TILES, 16, 128), F32),
            pltpu.VMEM((LEAVES + 1, 16, 64), F32),
            pltpu.VMEM((512, 256), F32),
            pltpu.SemaphoreType.DMA((15,)),
        ],
        compiler_params=pltpu.CompilerParams(vmem_limit_bytes=48 * 1024 * 1024),
        name="local",
    )(*inputs)


def body(
    right_sides,
    positions,
    point_order,
    leaf_basis,
    transfer,
    couple_local,
    partner_local,
    transfer_up,
    couple_up,
    partner_up,
    send_list,
    side_list,
    pair_target,
    pair_source,
    pair_count,
):
    order = point_order.reshape(1, POINTS)
    table, pool, upper, edges, edges_up, cup, blocks, codes = exchange(
        right_sides, positions, order, leaf_basis, transfer, transfer_up,
        couple_up.transpose(1, 0, 2), couple_local.transpose(1, 0, 2), partner_local.T, send_list[0], side_list[0],
    )
    return local(
        table, pair_target, pair_source, pair_count, positions, pool.reshape(GROUP * TILES, 16, 128), blocks, codes,
        upper, edges_up, cup, partner_up.T, edges, leaf_basis, order,
    )


def solution(mesh):
    placed = (
        P(None, ("branch", "row", "top")),
        P(None, ("branch", "row", "top")),
        P(("branch", "row", "top")),
        P(None, ("branch", "row", "top")),
        P(("branch", "row", "top"), None),
        P(("branch", "row", "top"), None, None),
        P(("branch", "row", "top"), None),
        P(),
        P("top", None, None),
        P(),
        P(("branch", "row", "top"), None, None),
        P(("branch", "row", "top"), None, None),
        P(("branch", "row", "top"), None),
        P(("branch", "row", "top"), None),
        P(("branch", "row", "top")),
    )
    return jax.shard_map(
        body,
        mesh=mesh,
        in_specs=placed,
        out_specs=P(None, ("branch", "row", "top")),
        check_vma=False,
    )
```

time: 164 us -> 80.8 us (0.49)
  the two profiles are of different devices: /device:TPU:15 before, /device:TPU:66 now
where the time goes in v1:
time: 80.8 us; the launch traced here: 80.3 us
  Pallas kernels  70.1 us (87%)
  local copies, waits for them, and re-layouts  9.49 us (12%)
    pallas_call x1, Pallas kernels, exchange(): pl.pallas_call(exchange_kernel, out_shape=(shape((2 * LEAVES + 2 * HALO,...  40.1 us
    pallas_call x1, Pallas kernels, local(): pl.pallas_call(local_kernel, out_shape=jax.ShapeDtypeStruct((NRHS, POINTS...  30 us
    unnamed x28, local copies, waits for them, and re-layouts  9.49 us

profile of v1, /device:TPU:66, one launch (start us, length us, event | category | flops | bytes accessed | tf_op | source)
XLA Modules:
  0.0 80.3 jit_solution(4315298208923685772)
XLA Ops:
  0.7 0.0 copy-start
  0.7 1.0 %copy-done = bf16[32,8192]{1,0:T(8,128)(2,1)S(1)} copy-done((bf16[32,8192]{1,0:T(8,128)(2,1)S(1)}, bf16[32,8192]{1,0:T(8,128)(2,1)}, u32[]{:S(2)}) %copy-start) | copy-done | bytes 524312
  1.7 0.0 copy-start.3
  1.7 1.2 %copy-done.3 = bf16[496,1024]{1,0:T(8,128)(2,1)S(1)} copy-done((bf16[496,1024]{1,0:T(8,128)(2,1)S(1)}, bf16[496,1024]{1,0:T(8,128)(2,1)}, u32[]{:S(2)}) %copy-start.3) | copy-done | bytes 1015832
  2.9 0.0 copy-start.4
  2.9 1.0 %copy-done.4 = bf16[254,1024]{1,0:T(8,128)(2,1)S(1)} copy-done((bf16[254,1024]{1,0:T(8,128)(2,1)S(1)}, bf16[254,1024]{1,0:T(8,128)(2,1)}, u32[]{:S(2)}) %copy-start.4) | copy-done | bytes 520216
  4.0 0.0 copy-start.5
  4.0 0.8 %copy-done.5 = bf16[3,8192]{1,0:T(4,128)(2,1)S(1)} copy-done((bf16[3,8192]{1,0:T(4,128)(2,1)S(1)}, bf16[3,8192]{1,0:T(4,128)(2,1)}, u32[]{:S(2)}) %copy-start.5) | copy-done | bytes 49176
  4.8 0.0 copy-start.6
  4.8 0.9 %copy-done.6 = bf16[16,8192]{1,0:T(8,128)(2,1)S(1)} copy-done((bf16[16,8192]{1,0:T(8,128)(2,1)S(1)}, bf16[16,8192]{1,0:T(8,128)(2,1)}, u32[]{:S(2)}) %copy-start.6) | copy-done | bytes 262168
  5.7 0.0 copy-start.7
  5.7 0.8 copy-done.7
  6.5 0.0 copy-start.9
  6.5 0.7 copy-done.9
  7.2 0.0 copy-start.10
  7.2 0.7 copy-done.10
  7.9 0.0 copy-start.13
  7.9 0.7 copy-done.13
  8.6 0.0 copy-start.1
  8.6 0.0 copy-start.8
  8.6 0.0 copy-start.11
  8.6 0.0 copy-start.12
  8.6 40.1 %exchange.1 = (bf16[320,16,128]{2,1,0:T(8,128)(2,1)S(1)}, bf16[8,64,16,128]{3,2,1,0:T(8,128)(2,1)}, bf16[32,4,16,128]{3,2,1,0:T(8,128)(2,1)S(1)}, bf16[8192,128]...) custom-call(bf16[16,8192]{1,0:T(8,128)(2,1)S(1)} %copy-done.6, ...), custom_call_target="tpu_custom_call" | custom-call | tf_op jit(solution)/shard_map/exchange/pallas_call | solution.py:483
  48.7 0.0 copy-done.1
  48.7 0.0 copy-done.8
  48.7 0.0 copy-done.11
  48.7 0.0 copy-done.12
  48.7 0.0 copy-start.2
  48.8 1.6 %copy-done.2 = bf16[8,64,16,128]{3,2,1,0:T(8,128)(2,1)S(1)} copy-done((bf16[8,64,16,128]{3,2,1,0:T(8,128)(2,1)S(1)}, bf16[8,64,16,128]{3,2,1,0:T(8,128)(2,1)}, u32[]{:S(2)}) %copy-start.2) | copy-done | bytes 2097176
  50.3 30.0 %local.1 = f32[16,8192]{1,0:T(8,128)} custom-call(bf16[320,16,128]{2,1,0:T(8,128)(2,1)S(1)} %get-tuple-element.13.table_h, s32[1,1024]{1,0:T(1,128)S(1)} %copy-done.11, s32[1,1024]{1,0:T(1,128)S(1)} %copy-done.12, s32[1]{0:T(128)S(6)} %copy.16.count_h, bf16[3,8192]{1,0:T(4,128)(2,1)S(1)} %copy-done.5, bf16[512,16,128]{2,1,0:T(8,128)(2,1)S(1)} %bitcast.8, ...), custom_call_target="tpu_custom_call" | custom-call | tf_op jit(solution)/shard_map/local/pallas_call | solution.py:768
Async XLA Ops:
  0.7 1.0 %copy-start = (bf16[32,8192]{1,0:T(8,128)(2,1)S(1)}, bf16[32,8192]{1,0:T(8,128)(2,1)}, u32[]{:S(2)}) copy-start(bf16[32,8192]{1,0:T(8,128)(2,1)} %basis_h.3) | copy-start | bytes 1572868
  1.7 1.2 %copy-start.3 = (bf16[496,1024]{1,0:T(8,128)(2,1)S(1)}, bf16[496,1024]{1,0:T(8,128)(2,1)}, u32[]{:S(2)}) copy-start(bf16[496,1024]{1,0:T(8,128)(2,1)} %tup_h.1) | copy-start | bytes 3047428
  2.9 1.0 %copy-start.4 = (bf16[254,1024]{1,0:T(8,128)(2,1)S(1)}, bf16[254,1024]{1,0:T(8,128)(2,1)}, u32[]{:S(2)}) copy-start(bf16[254,1024]{1,0:T(8,128)(2,1)} %trans_h.1) | copy-start | bytes 1560580
  4.0 0.8 %copy-start.5 = (bf16[3,8192]{1,0:T(4,128)(2,1)S(1)}, bf16[3,8192]{1,0:T(4,128)(2,1)}, u32[]{:S(2)}) copy-start(bf16[3,8192]{1,0:T(4,128)(2,1)} %xyz_h.3) | copy-start | bytes 147460
  4.8 0.9 %copy-start.6 = (bf16[16,8192]{1,0:T(8,128)(2,1)S(1)}, bf16[16,8192]{1,0:T(8,128)(2,1)}, u32[]{:S(2)}) copy-start(bf16[16,8192]{1,0:T(8,128)(2,1)} %rhs_h.1) | copy-start | bytes 786436
  5.7 0.8 copy-start.7
  6.5 0.7 copy-start.9
  7.2 0.7 copy-start.10
  7.9 0.7 copy-start.13
  8.6 40.1 %copy-start.1 = (bf16[32,8192]{1,0:T(8,128)(2,1)S(1)}, bf16[32,8192]{1,0:T(8,128)(2,1)}, u32[]{:S(2)}) copy-start(bf16[32,8192]{1,0:T(8,128)(2,1)} %basis_h.3) | copy-start | bytes 1572868
  8.6 40.1 %copy-start.8 = (s32[504,6]{0,1:T(8,128)S(1)}, s32[504,6]{0,1:T(8,128)}, u32[]{:S(2)}) copy-start(s32[504,6]{0,1:T(8,128)} %param.24) | copy-start | bytes 36292
  8.6 40.2 %copy-start.11 = (s32[1,1024]{1,0:T(1,128)S(1)}, s32[1,1024]{1,0:T(1,128)}, u32[]{:S(2)}) copy-start(s32[1,1024]{1,0:T(1,128)} %target_h.1) | copy-start | bytes 12292
  8.6 40.2 %copy-start.12 = (s32[1,1024]{1,0:T(1,128)S(1)}, s32[1,1024]{1,0:T(1,128)}, u32[]{:S(2)}) copy-start(s32[1,1024]{1,0:T(1,128)} %source_h.1) | copy-start | bytes 12292
  48.7 1.6 %copy-start.2 = (bf16[8,64,16,128]{3,2,1,0:T(8,128)(2,1)S(1)}, bf16[8,64,16,128]{3,2,1,0:T(8,128)(2,1)}, u32[]{:S(2)}) copy-start(bf16[8,64,16,128]{3,2,1,0:T(8,128)(2,1)} %get-tuple-element.14) | copy-start | bytes 6291460

commit v2 on v1

--- a/solution.py
+++ b/solution.py
@@ -19,6 +19,7 @@
 UPPER = 504
 LEVELS = 7
 TILES = 64
+PITCH = 33
 
 INV_FOUR_PI = 0.07957747154594767
 SOFTENING = 0.01
@@ -135,7 +136,7 @@
     held = (rhs, xyz, order, basis, trans, tup, cup, couple, partner, send_s, side_s)
     given = (rhs_h, xyz_h, order_h, basis_h, trans_h, tup_h, cup_h, couple_h, partner_h, send_h, side_h)
     fetched = [pltpu.make_async_copy(a, b, in_sem.at[i]) for i, (a, b) in enumerate(zip(given, held))]
-    for i in (0, 2, 1, 3, 9, 10, 4, 5, 6, 7, 8):
+    for i in (4, 0, 2, 1, 3, 9, 10, 5, 6, 8, 7):
         fetched[i].start()
 
     def member(index):
@@ -156,6 +157,31 @@
         return carry
 
     lax.fori_loop(1, BRANCHES, greet, 0)
+
+    fetched[4].wait()
+    tail_s[...] = jnp.zeros((16, 1024), F32)
+    tail_s[0:14, :] = trans[240:254, :].astype(F32)
+
+    def spread_one(rows_of, start, part):
+        def put(p, out):
+            edge_s[part, pl.ds(p, 16, stride=PITCH), :] = out
+
+        spread_edges(rows_of, put)
+        for u in range(16):
+            rows = pl.ds(pl.multiple_of(start + 32 * u, 32), 32)
+            edges[rows, :] = edge_s[part, PITCH * u : PITCH * u + 32].astype(BF)
+
+    def spread(c, carry):
+        for part in range(3):
+            start = pl.multiple_of(48 * c + 16 * part, 16)
+            spread_one(
+                lambda g: trans[pl.ds(start, 16), 128 * g : 128 * g + 128].astype(F32),
+                1536 * c + 512 * part, part,
+            )
+        return carry
+
+    lax.fori_loop(0, 5, spread, 0)
+    spread_one(lambda g: tail_s[:, 128 * g : 128 * g + 128], 7680, 0)
 
     for i in range(4):
         fetched[i].wait()
@@ -193,140 +219,6 @@
 
     lax.fori_loop(0, 16, chunk, 0, unroll=2)
 
-    fetched[9].wait()
-    fetched[10].wait()
-
-    def fill(k, carry):
-        for m in range(GROUP):
-            near_s[m, k] = table_s[send_s[m, k]]
-        for s in range(2):
-            side_buf[s, 2 * k] = table_s[side_s[s, 2 * k]]
-            side_buf[s, 2 * k + 1] = table_s[side_s[s, 2 * k + 1]]
-        return carry
-
-    lax.fori_loop(0, SLOT, fill, 0)
-
-    pl.semaphore_wait(barrier, GROUP - 1 + BRANCHES - 1)
-
-    sent = []
-
-    def send(src, dst, send_sem, recv_sem, device_id):
-        copy = pltpu.make_async_remote_copy(
-            src_ref=src, dst_ref=dst, send_sem=send_sem, recv_sem=recv_sem,
-            device_id=device_id, device_id_type=MESH,
-        )
-        copy.start()
-        sent.append(copy)
-        return copy
-
-    kept = []
-
-    def keep(src, dst, sem):
-        copy = pltpu.make_async_copy(src, dst, sem)
-        copy.start()
-        kept.append(copy)
-
-    partner_core = (branch, row, 1 - top)
-    next_row = (branch, (row + 1) % 4, top)
-    last_row = (branch, (row + 3) % 4, top)
-    before = ((row + 3) % 4) * 2 + top
-    after = ((row + 1) % 4) * 2 + top
-    across = ((row + 2) % 4) * 2 + top
-
-    def ring_first(p, src):
-        tiles = pl.ds(32 * p, 32)
-        one = send(src, pool_o.at[me, tiles], ring_send.at[4 * p], ring_recv.at[4 * p], next_row)
-        two = send(src, pool_o.at[me, tiles], ring_send.at[4 * p + 1], ring_recv.at[4 * p + 1], last_row)
-        core = send(src, pool_o.at[me, tiles], core_send.at[5 * p], core_recv.at[5 * p], partner_core)
-        return one, two, core
-
-    def ring_second(p, first):
-        tiles = pl.ds(32 * p, 32)
-        first[0].wait_recv()
-        lower = pl.ds(32 * p, 16)
-        three = send(
-            pool_o.at[before, lower], pool_o.at[before, lower],
-            ring_send.at[4 * p + 2], ring_recv.at[4 * p + 2], next_row,
-        )
-        a = send(
-            pool_o.at[before, tiles], pool_o.at[before, tiles],
-            core_send.at[5 * p + 1], core_recv.at[5 * p + 1], partner_core,
-        )
-        first[1].wait_recv()
-        higher = pl.ds(32 * p + 16, 16)
-        four = send(
-            pool_o.at[after, higher], pool_o.at[after, higher],
-            ring_send.at[4 * p + 3], ring_recv.at[4 * p + 3], last_row,
-        )
-        b = send(
-            pool_o.at[after, tiles], pool_o.at[after, tiles],
-            core_send.at[5 * p + 2], core_recv.at[5 * p + 2], partner_core,
-        )
-        return three, four, a, b
-
-    def ring_third(p, second):
-        second[0].wait_recv()
-        lower = pl.ds(32 * p, 16)
-        a = send(
-            pool_o.at[across, lower], pool_o.at[across, lower],
-            core_send.at[5 * p + 3], core_recv.at[5 * p + 3], partner_core,
-        )
-        second[1].wait_recv()
-        higher = pl.ds(32 * p + 16, 16)
-        b = send(
-            pool_o.at[across, higher], pool_o.at[across, higher],
-            core_send.at[5 * p + 4], core_recv.at[5 * p + 4], partner_core,
-        )
-        return a, b
-
-    leaves_first = ring_first(0, pool_s.at[pl.ds(0, 32)])
-    arriving = [leaves_first[2]]
-    for offset in range(1, GROUP):
-        arriving.append(
-            send(
-                near_s.at[peer(offset)], table_o.at[pl.ds(LEAVES + me * SLOT, SLOT)],
-                near_send.at[offset - 1], near_recv.at[offset - 1], member(peer(offset)),
-            )
-        )
-    arriving.append(
-        send(
-            side_buf.at[1], table_o.at[pl.ds(2 * LEAVES, HALO)],
-            near_send.at[7], near_recv.at[7], cousin(1),
-        )
-    )
-    arriving.append(
-        send(
-            side_buf.at[0], table_o.at[pl.ds(2 * LEAVES + HALO, HALO)],
-            near_send.at[8], near_recv.at[8], cousin(BRANCHES - 1),
-        )
-    )
-    keep(table_s, table_o.at[pl.ds(0, LEAVES)], local_sem.at[0])
-    keep(near_s.at[me], table_o.at[pl.ds(LEAVES + me * SLOT, SLOT)], local_sem.at[1])
-
-    fetched[4].wait()
-    tail_s[...] = jnp.zeros((16, 1024), F32)
-    tail_s[0:14, :] = trans[240:254, :].astype(F32)
-
-    def spread_one(rows_of, start, part):
-        def put(p, out):
-            edge_s[part, pl.ds(p, 16, stride=32), :] = out
-
-        spread_edges(rows_of, put)
-        edges[pl.ds(start, 512), :] = edge_s[part, 0:512].astype(BF)
-
-    def spread(c, carry):
-        for part in range(3):
-            start = pl.multiple_of(48 * c + 16 * part, 16)
-            spread_one(
-                lambda g: trans[pl.ds(start, 16), 128 * g : 128 * g + 128].astype(F32),
-                pl.multiple_of(1536 * c + 512 * part, 512), part,
-            )
-        return carry
-
-    lax.fori_loop(0, 5, spread, 0)
-    spread_one(lambda g: tail_s[:, 128 * g : 128 * g + 128], 7680, 0)
-    keep(edges, edges_o, local_sem.at[4])
-
     tile_of = [first_row(level) // 4 for level in range(LEVELS)]
     for level in range(LEVELS - 2):
         for t in range((LEAVES >> level) // 8):
@@ -342,6 +234,79 @@
     for k in (0, 1, 3):
         placed = jnp.where(me % 4 == k, pltpu.roll(root, (32 * (k - 2)) % 128, 1), placed)
     root_s[...] = placed.astype(BF)
+    pl.semaphore_wait(barrier, GROUP - 1 + BRANCHES - 1)
+
+    sent = []
+
+    def send(src, dst, send_sem, recv_sem, device_id):
+        copy = pltpu.make_async_remote_copy(
+            src_ref=src, dst_ref=dst, send_sem=send_sem, recv_sem=recv_sem,
+            device_id=device_id, device_id_type=MESH,
+        )
+        copy.start()
+        sent.append(copy)
+        return copy
+
+    kept = []
+
+    def keep(src, dst, sem):
+        copy = pltpu.make_async_copy(src, dst, sem)
+        copy.start()
+        kept.append(copy)
+
+    partner_core = (branch, row, 1 - top)
+    next_row = (branch, (row + 1) % 4, top)
+    last_row = (branch, (row + 3) % 4, top)
+    before = ((row + 3) % 4) * 2 + top
+    after = ((row + 1) % 4) * 2 + top
+    across = ((row + 2) % 4) * 2 + top
+
+    def ring_first(p, src):
+        tiles = pl.ds(32 * p, 32)
+        one = send(src, pool_o.at[me, tiles], ring_send.at[4 * p], ring_recv.at[4 * p], next_row)
+        two = send(src, pool_o.at[me, tiles], ring_send.at[4 * p + 1], ring_recv.at[4 * p + 1], last_row)
+        core = send(src, pool_o.at[me, tiles], core_send.at[5 * p], core_recv.at[5 * p], partner_core)
+        return one, two, core
+
+    def ring_second(p, first):
+        tiles = pl.ds(32 * p, 32)
+        first[0].wait_recv()
+        lower = pl.ds(32 * p, 16)
+        three = send(
+            pool_o.at[before, lower], pool_o.at[before, lower],
+            ring_send.at[4 * p + 2], ring_recv.at[4 * p + 2], next_row,
+        )
+        a = send(
+            pool_o.at[before, tiles], pool_o.at[before, tiles],
+            core_send.at[5 * p + 1], core_recv.at[5 * p + 1], partner_core,
+        )
+        first[1].wait_recv()
+        higher = pl.ds(32 * p + 16, 16)
+        four = send(
+            pool_o.at[after, higher], pool_o.at[after, higher],
+            ring_send.at[4 * p + 3], ring_recv.at[4 * p + 3], last_row,
+        )
+        b = send(
+            pool_o.at[after, tiles], pool_o.at[after, tiles],
+            core_send.at[5 * p + 2], core_recv.at[5 * p + 2], partner_core,
+        )
+        return three, four, a, b
+
+    def ring_third(p, second):
+        second[0].wait_recv()
+        lower = pl.ds(32 * p, 16)
+        a = send(
+            pool_o.at[across, lower], pool_o.at[across, lower],
+            core_send.at[5 * p + 3], core_recv.at[5 * p + 3], partner_core,
+        )
+        second[1].wait_recv()
+        higher = pl.ds(32 * p + 16, 16)
+        b = send(
+            pool_o.at[across, higher], pool_o.at[across, higher],
+            core_send.at[5 * p + 4], core_recv.at[5 * p + 4], partner_core,
+        )
+        return a, b
+
     roots = []
     for offset in range(1, GROUP):
         roots.append(
@@ -351,11 +316,47 @@
             )
         )
     roots_s[me] = root_s[...]
+    leaves_first = ring_first(0, pool_s.at[pl.ds(0, 32)])
+    arriving = [leaves_first[2]]
+    fetched[9].wait()
+    fetched[10].wait()
+
+    def fill(k, carry):
+        for m in range(GROUP):
+            near_s[m, k] = table_s[send_s[m, k]]
+        for s in range(2):
+            side_buf[s, 2 * k] = table_s[side_s[s, 2 * k]]
+            side_buf[s, 2 * k + 1] = table_s[side_s[s, 2 * k + 1]]
+        return carry
+
+    lax.fori_loop(0, SLOT, fill, 0)
+
+    for offset in range(1, GROUP):
+        arriving.append(
+            send(
+                near_s.at[peer(offset)], table_o.at[pl.ds(LEAVES + me * SLOT, SLOT)],
+                near_send.at[offset - 1], near_recv.at[offset - 1], member(peer(offset)),
+            )
+        )
+    arriving.append(
+        send(
+            side_buf.at[1], table_o.at[pl.ds(2 * LEAVES, HALO)],
+            near_send.at[7], near_recv.at[7], cousin(1),
+        )
+    )
+    arriving.append(
+        send(
+            side_buf.at[0], table_o.at[pl.ds(2 * LEAVES + HALO, HALO)],
+            near_send.at[8], near_recv.at[8], cousin(BRANCHES - 1),
+        )
+    )
+    keep(table_s, table_o.at[pl.ds(0, LEAVES)], local_sem.at[0])
+    keep(near_s.at[me], table_o.at[pl.ds(LEAVES + me * SLOT, SLOT)], local_sem.at[1])
+
     rest_first = ring_first(1, pool_s.at[pl.ds(32, 32)])
     arriving.append(rest_first[2])
     keep(pool_s, pool_o.at[me], local_sem.at[2])
-    leaves_second = ring_second(0, leaves_first)
-    arriving += leaves_second[2:]
+    keep(edges, edges_o, local_sem.at[4])
 
     fetched[5].wait()
     slot = iota((64, 496), 0)
@@ -371,10 +372,11 @@
     chosen = dot((iota((64, 496), 1) == want).astype(F32).astype(BF), tup[...])
 
     def put_up(p, out):
-        edge_s[0, pl.ds(p, 64, stride=32), :] = out
+        edge_s[0, pl.ds(p, 64, stride=PITCH), :] = out
 
     spread_edges(lambda g: chosen[:, 128 * g : 128 * g + 128], put_up)
-    edges_up[...] = edge_s[0].astype(BF)
+    for u in range(64):
+        edges_up[32 * u : 32 * u + 32, :] = edge_s[0, PITCH * u : PITCH * u + 32].astype(BF)
     keep(edges_up, edges_up_o, local_sem.at[5])
 
     for copy in roots:
@@ -425,6 +427,9 @@
     codes[:, 0:254] = (partner[...] >> width) * 256 + start + (partner[...] & ((1 << width) - 1))
     keep(codes, codes_o, local_sem.at[6])
 
+    leaves_second = ring_second(0, leaves_first)
+    arriving += leaves_second[2:]
+
     fetched[7].wait()
     for f in range(FAR):
         block_tail[f] = jnp.zeros((16, 1024), F32)
@@ -432,30 +437,34 @@
 
     def couple_one(rows_of, start, part):
         def put(a, low, high):
-            block_s[part, 0, pl.ds(a, 16, stride=32), :] = low
-            block_s[part, 1, pl.ds(a, 16, stride=32), :] = high
+            block_s[part, 0, pl.ds(a, 16, stride=PITCH), :] = low
+            block_s[part, 1, pl.ds(a, 16, stride=PITCH), :] = high
 
         spread_blocks(rows_of, put)
-        blocks[pl.ds(start, 512), 0:128] = block_s[part, 0].astype(BF)
-        blocks[pl.ds(start, 512), 128:256] = block_s[part, 1].astype(BF)
+        for half in range(2):
+            for u in range(16):
+                rows = pl.ds(pl.multiple_of(start + 32 * u, 32), 32)
+                blocks[rows, 128 * half : 128 * half + 128] = block_s[
+                    part, half, PITCH * u : PITCH * u + 32
+                ].astype(BF)
 
     def couple_rows(c, carry):
         start = pl.multiple_of(16 * c, 16)
         couple_one(
             lambda f, g: couple[f, pl.ds(start, 16), 128 * g : 128 * g + 128].astype(F32),
-            pl.multiple_of(512 * c, 512), 0,
+            512 * c, 0,
         )
         return carry
 
     lax.fori_loop(0, 8, couple_rows, 0)
+    lax.fori_loop(8, 15, couple_rows, 0)
     rest_second = ring_second(1, rest_first)
     arriving += rest_second[2:]
-    arriving += ring_third(0, leaves_second)
-    lax.fori_loop(8, 15, couple_rows, 0)
-    arriving += ring_third(1, rest_second)
     couple_one(lambda f, g: block_tail[f, :, 128 * g : 128 * g + 128], 7680, 0)
     keep(blocks, blocks_o, local_sem.at[7])
 
+    arriving += ring_third(0, leaves_second)
+    arriving += ring_third(1, rest_second)
     cup_copy.wait_recv()
     cup_own[...] = cup_own[...] + cup_recv[...]
     keep(cup_own, cup_o, local_sem.at[8])
@@ -500,7 +509,7 @@
             pltpu.VMEM((512, 256), BF),
             pltpu.VMEM((LEAVES, 16, 128), BF),
             pltpu.VMEM((TILES, 16, 128), BF),
-            pltpu.VMEM((3, 2048, 128), F32),
+            pltpu.VMEM((3, 64 * PITCH, 128), F32),
             pltpu.VMEM((16, 1024), F32),
             pltpu.VMEM((GROUP, SLOT, 16, 128), BF),
             pltpu.VMEM((2, HALO, 16, 128), BF),
@@ -512,7 +521,7 @@
             pltpu.VMEM((FAR, 8, 1024), F32),
             pltpu.VMEM((8192, 128), BF),
             pltpu.VMEM((2048, 128), BF),
-            pltpu.VMEM((1, 2, 512, 128), F32),
+            pltpu.VMEM((1, 2, 16 * PITCH, 128), F32),
             pltpu.VMEM((FAR, 16, 1024), F32),
             pltpu.VMEM((8192, 256), BF),
             pltpu.VMEM((FAR, 256), I32),
@@ -522,7 +531,7 @@
             for count in (11, 9, 9, 10, 10, 8, 8, 7, 7, BRANCHES - 1, BRANCHES - 1, 2, 9)
         ],
         compiler_params=pltpu.CompilerParams(
-            collective_id=0, has_side_effects=True, vmem_limit_bytes=48 * 1024 * 1024
+            collective_id=0, has_side_effects=True, vmem_limit_bytes=64 * 1024 * 1024
         ),
         name="exchange",
     )(*inputs)
@@ -539,10 +548,9 @@
              edges_h, basis_h, order_h)
     held = (table, target, source, count, xyz, pool, blocks, codes, upper, edges_up, cup, pup, edges, basis, order)
     fetched = [pltpu.make_async_copy(a, b, in_sem.at[i]) for i, (a, b) in enumerate(zip(given, held))]
-    for copy in fetched:
-        copy.start()
-    for copy in fetched[:5]:
-        copy.wait()
+    for i in (4, 0, 1, 2, 3, 5, 6, 7, 8, 9, 10, 11, 12, 13, 14):
+        fetched[i].start()
+    fetched[4].wait()
     branch = lax.axis_index("branch")
     me = lax.axis_index("row") * 2 + lax.axis_index("top")
     device = branch * GROUP + me
@@ -561,18 +569,21 @@
 
     lax.fori_loop(0, 64, goals, 0, unroll=16)
 
+    def clear(t, carry):
+        near_s[t] = jnp.zeros((16, 64), F32)
+        return carry
+
+    lax.fori_loop(0, LEAVES + 1, clear, 0, unroll=3)
+
+    for copy in fetched[:4]:
+        copy.wait()
+
     def swaps(c, carry):
         tiles = table[pl.ds(8 * c, 8)].reshape(128, 128).astype(F32)
         swap_s[pl.ds(8 * c, 8)] = pltpu.roll(tiles, 64, 1).astype(BF).reshape(8, 16, 128)
         return carry
 
     lax.fori_loop(0, 40, swaps, 0, unroll=4)
-
-    def clear(t, carry):
-        near_s[t] = jnp.zeros((16, 64), F32)
-        return carry
-
-    lax.fori_loop(0, LEAVES + 1, clear, 0, unroll=3)
 
     live = count[0]
     lane16 = (iota((64, 64), 1) >> 4)
@@ -785,7 +796,7 @@
             pltpu.VMEM((512, 256), F32),
             pltpu.SemaphoreType.DMA((15,)),
         ],
-        compiler_params=pltpu.CompilerParams(vmem_limit_bytes=48 * 1024 * 1024),
+        compiler_params=pltpu.CompilerParams(vmem_limit_bytes=64 * 1024 * 1024),
         name="local",
     )(*inputs)
 

time: 80.8 us -> 67 us (0.83)
  the two profiles are of different devices: /device:TPU:66 before, /device:TPU:1 now
where the time goes in v2:
time: 67 us; the launch traced here: 66.9 us
  Pallas kernels  66.2 us (99%)
    pallas_call x1, Pallas kernels, exchange(): pl.pallas_call(exchange_kernel, out_shape=(shape((2 * LEAVES + 2 * HALO,...  36.2 us
    pallas_call x1, Pallas kernels, local(): pl.pallas_call(local_kernel, out_shape=jax.ShapeDtypeStruct((NRHS, POINTS...  30.1 us

profile of v2, /device:TPU:1, one launch (start us, length us, event | category | flops | bytes accessed | tf_op | source)
XLA Modules:
  0.0 66.9 jit_solution(1579460647053031625)
XLA Ops:
  0.7 36.2 %exchange.1 = (bf16[320,16,128]{2,1,0:T(8,128)(2,1)}, bf16[8,64,16,128]{3,2,1,0:T(8,128)(2,1)}, bf16[32,4,16,128]{3,2,1,0:T(8,128)(2,1)}, bf16[8192,128]{1,0:T(8...) custom-call(bf16[16,8192]{1,0:T(8,128)(2,1)} %rhs_h.1, ...), custom_call_target="tpu_custom_call" | custom-call | tf_op jit(solution)/shard_map/exchange/pallas_call | solution.py:492
  36.8 30.1 %local.1 = f32[16,8192]{1,0:T(8,128)} custom-call(bf16[320,16,128]{2,1,0:T(8,128)(2,1)} %get-tuple-element.13.table_h, s32[1,1024]{1,0:T(1,128)} %target_h.1, s32[1,1024]{1,0:T(1,128)} %source_h.1, s32[1]{0:T(128)S(6)} %copy.16.count_h, bf16[3,8192]{1,0:T(4,128)(2,1)} %xyz_h.3, bf16[512,16,128]{2,1,0:T(8,128)(2,1)} %bitcast.10, ...), custom_call_target="tpu_custom_call" | custom-call | tf_op jit(solution)/shard_map/local/pallas_call | solution.py:779

commit v3 on v2

--- a/solution.py
+++ b/solution.py
@@ -20,6 +20,8 @@
 LEVELS = 7
 TILES = 64
 PITCH = 33
+RECEIVED = GROUP * SLOT + 2 * HALO
+OWN = 832
 
 INV_FOUR_PI = 0.07957747154594767
 SOFTENING = 0.01
@@ -118,12 +120,41 @@
     return jnp.concatenate([jnp.where(lane == j, basis, zero) for j in range(4)], axis=0)
 
 
+def near_quad(goals, table, swapped, at, to, left):
+    zero = jnp.zeros((16, 128), BF)
+    lane16 = iota((64, 64), 1) >> 4
+    g = [goals[to[i]] for i in range(4)]
+    lhs = jnp.where(lane16 == 0, g[0], jnp.where(lane16 == 1, g[1], jnp.where(lane16 == 2, g[2], g[3])))
+    value, other = [], []
+    for i in range(4):
+        plain, turned = table[at[i]], swapped[at[i]]
+        if i % 2 == 0:
+            pieces = [jnp.where(left, plain, zero), jnp.where(left, turned, zero)]
+        else:
+            pieces = [jnp.where(left, zero, turned), jnp.where(left, zero, plain)]
+        for rows, piece in zip((value, other), pieces):
+            rows.append(jnp.concatenate([piece, zero] if i < 2 else [zero, piece], axis=1))
+    tile = lax.rsqrt(dot(lhs, jnp.concatenate(other, axis=0))).astype(BF)
+    wide = dot_nt(jnp.concatenate(value, axis=0), tile)
+    return [wide[16 * i : 16 * i + 16] for i in range(4)]
+
+
+def swap_halves(table, swapped, count):
+    def swap(c, carry):
+        tiles = table[pl.ds(8 * c, 8)].reshape(128, 128).astype(F32)
+        swapped[pl.ds(8 * c, 8)] = pltpu.roll(tiles, 64, 1).astype(BF).reshape(8, 16, 128)
+        return carry
+
+    lax.fori_loop(0, count // 8, swap, 0, unroll=4)
+
+
 def exchange_kernel(
     rhs_h, xyz_h, order_h, basis_h, trans_h, tup_h, cup_h, couple_h, partner_h, send_h, side_h,
-    table_o, pool_o, upper_o, edges_o, edges_up_o, cup_o, blocks_o, codes_o,
-    rhs, xyz, order, basis, trans, tup, cup, couple, partner, send_s, side_s,
+    target_h, source_h,
+    table_o, pool_o, upper_o, edges_o, edges_up_o, cup_o, blocks_o, codes_o, goals_o, terms_o,
+    rhs, xyz, order, basis, trans, tup, cup, couple, partner, send_s, side_s, target, source,
     x_s, table_s, pool_s, edge_s, tail_s, near_s, side_buf, root_s, roots_s, upper_s, cup_own, cup_send, cup_recv,
-    edges, edges_up, block_s, block_tail, blocks, codes,
+    edges, edges_up, block_s, block_tail, blocks, codes, goals_s, swap_s, terms,
     in_sem, near_send, near_recv, core_send, core_recv, ring_send, ring_recv,
     root_send, root_recv, up_send, up_recv, cup_sem, local_sem,
 ):
@@ -133,10 +164,11 @@
     me = row * 2 + top
     device = branch * GROUP + me
 
-    held = (rhs, xyz, order, basis, trans, tup, cup, couple, partner, send_s, side_s)
-    given = (rhs_h, xyz_h, order_h, basis_h, trans_h, tup_h, cup_h, couple_h, partner_h, send_h, side_h)
+    held = (rhs, xyz, order, basis, trans, tup, cup, couple, partner, send_s, side_s, target, source)
+    given = (rhs_h, xyz_h, order_h, basis_h, trans_h, tup_h, cup_h, couple_h, partner_h, send_h, side_h,
+             target_h, source_h)
     fetched = [pltpu.make_async_copy(a, b, in_sem.at[i]) for i, (a, b) in enumerate(zip(given, held))]
-    for i in (4, 0, 2, 1, 3, 9, 10, 5, 6, 8, 7):
+    for i in (4, 0, 2, 1, 3, 9, 10, 5, 6, 8, 7, 11, 12):
         fetched[i].start()
 
     def member(index):
@@ -217,7 +249,86 @@
             ).astype(BF)
         return carry
 
-    lax.fori_loop(0, 16, chunk, 0, unroll=2)
+    lax.fori_loop(0, 8, chunk, 0, unroll=2)
+    pl.semaphore_wait(barrier, GROUP - 1 + BRANCHES - 1)
+
+    sent = []
+
+    def send(src, dst, send_sem, recv_sem, device_id):
+        copy = pltpu.make_async_remote_copy(
+            src_ref=src, dst_ref=dst, send_sem=send_sem, recv_sem=recv_sem,
+            device_id=device_id, device_id_type=MESH,
+        )
+        copy.start()
+        sent.append(copy)
+        return copy
+
+    kept = []
+
+    def keep(src, dst, sem):
+        copy = pltpu.make_async_copy(src, dst, sem)
+        copy.start()
+        kept.append(copy)
+
+    partner_core = (branch, row, 1 - top)
+    next_row = (branch, (row + 1) % 4, top)
+    last_row = (branch, (row + 3) % 4, top)
+    before = ((row + 3) % 4) * 2 + top
+    after = ((row + 1) % 4) * 2 + top
+    across = ((row + 2) % 4) * 2 + top
+
+    parts = ((0, 16), (16, 16), (32, 32))
+
+    def ring_first(p):
+        tiles = pl.ds(*parts[p])
+        src = pool_s.at[tiles]
+        one = send(src, pool_o.at[me, tiles], ring_send.at[4 * p], ring_recv.at[4 * p], next_row)
+        two = send(src, pool_o.at[me, tiles], ring_send.at[4 * p + 1], ring_recv.at[4 * p + 1], last_row)
+        core = send(src, pool_o.at[me, tiles], core_send.at[5 * p], core_recv.at[5 * p], partner_core)
+        return one, two, core
+
+    def ring_second(p, first):
+        tiles = pl.ds(*parts[p])
+        first[0].wait_recv()
+        lower = pl.ds(parts[p][0], parts[p][1] // 2)
+        three = send(
+            pool_o.at[before, lower], pool_o.at[before, lower],
+            ring_send.at[4 * p + 2], ring_recv.at[4 * p + 2], next_row,
+        )
+        a = send(
+            pool_o.at[before, tiles], pool_o.at[before, tiles],
+            core_send.at[5 * p + 1], core_recv.at[5 * p + 1], partner_core,
+        )
+        first[1].wait_recv()
+        higher = pl.ds(parts[p][0] + parts[p][1] // 2, parts[p][1] // 2)
+        four = send(
+            pool_o.at[after, higher], pool_o.at[after, higher],
+            ring_send.at[4 * p + 3], ring_recv.at[4 * p + 3], last_row,
+        )
+        b = send(
+            pool_o.at[after, tiles], pool_o.at[after, tiles],
+            core_send.at[5 * p + 2], core_recv.at[5 * p + 2], partner_core,
+        )
+        return three, four, a, b
+
+    def ring_third(p, second):
+        second[0].wait_recv()
+        lower = pl.ds(parts[p][0], parts[p][1] // 2)
+        a = send(
+            pool_o.at[across, lower], pool_o.at[across, lower],
+            core_send.at[5 * p + 3], core_recv.at[5 * p + 3], partner_core,
+        )
+        second[1].wait_recv()
+        higher = pl.ds(parts[p][0] + parts[p][1] // 2, parts[p][1] // 2)
+        b = send(
+            pool_o.at[across, higher], pool_o.at[across, higher],
+            core_send.at[5 * p + 4], core_recv.at[5 * p + 4], partner_core,
+        )
+        return a, b
+
+    first = [ring_first(0)]
+    lax.fori_loop(8, 16, chunk, 0, unroll=2)
+    first.append(ring_first(1))
 
     tile_of = [first_row(level) // 4 for level in range(LEVELS)]
     for level in range(LEVELS - 2):
@@ -234,79 +345,6 @@
     for k in (0, 1, 3):
         placed = jnp.where(me % 4 == k, pltpu.roll(root, (32 * (k - 2)) % 128, 1), placed)
     root_s[...] = placed.astype(BF)
-    pl.semaphore_wait(barrier, GROUP - 1 + BRANCHES - 1)
-
-    sent = []
-
-    def send(src, dst, send_sem, recv_sem, device_id):
-        copy = pltpu.make_async_remote_copy(
-            src_ref=src, dst_ref=dst, send_sem=send_sem, recv_sem=recv_sem,
-            device_id=device_id, device_id_type=MESH,
-        )
-        copy.start()
-        sent.append(copy)
-        return copy
-
-    kept = []
-
-    def keep(src, dst, sem):
-        copy = pltpu.make_async_copy(src, dst, sem)
-        copy.start()
-        kept.append(copy)
-
-    partner_core = (branch, row, 1 - top)
-    next_row = (branch, (row + 1) % 4, top)
-    last_row = (branch, (row + 3) % 4, top)
-    before = ((row + 3) % 4) * 2 + top
-    after = ((row + 1) % 4) * 2 + top
-    across = ((row + 2) % 4) * 2 + top
-
-    def ring_first(p, src):
-        tiles = pl.ds(32 * p, 32)
-        one = send(src, pool_o.at[me, tiles], ring_send.at[4 * p], ring_recv.at[4 * p], next_row)
-        two = send(src, pool_o.at[me, tiles], ring_send.at[4 * p + 1], ring_recv.at[4 * p + 1], last_row)
-        core = send(src, pool_o.at[me, tiles], core_send.at[5 * p], core_recv.at[5 * p], partner_core)
-        return one, two, core
-
-    def ring_second(p, first):
-        tiles = pl.ds(32 * p, 32)
-        first[0].wait_recv()
-        lower = pl.ds(32 * p, 16)
-        three = send(
-            pool_o.at[before, lower], pool_o.at[before, lower],
-            ring_send.at[4 * p + 2], ring_recv.at[4 * p + 2], next_row,
-        )
-        a = send(
-            pool_o.at[before, tiles], pool_o.at[before, tiles],
-            core_send.at[5 * p + 1], core_recv.at[5 * p + 1], partner_core,
-        )
-        first[1].wait_recv()
-        higher = pl.ds(32 * p + 16, 16)
-        four = send(
-            pool_o.at[after, higher], pool_o.at[after, higher],
-            ring_send.at[4 * p + 3], ring_recv.at[4 * p + 3], last_row,
-        )
-        b = send(
-            pool_o.at[after, tiles], pool_o.at[after, tiles],
-            core_send.at[5 * p + 2], core_recv.at[5 * p + 2], partner_core,
-        )
-        return three, four, a, b
-
-    def ring_third(p, second):
-        second[0].wait_recv()
-        lower = pl.ds(32 * p, 16)
-        a = send(
-            pool_o.at[across, lower], pool_o.at[across, lower],
-            core_send.at[5 * p + 3], core_recv.at[5 * p + 3], partner_core,
-        )
-        second[1].wait_recv()
-        higher = pl.ds(32 * p + 16, 16)
-        b = send(
-            pool_o.at[across, higher], pool_o.at[across, higher],
-            core_send.at[5 * p + 4], core_recv.at[5 * p + 4], partner_core,
-        )
-        return a, b
-
     roots = []
     for offset in range(1, GROUP):
         roots.append(
@@ -316,8 +354,7 @@
             )
         )
     roots_s[me] = root_s[...]
-    leaves_first = ring_first(0, pool_s.at[pl.ds(0, 32)])
-    arriving = [leaves_first[2]]
+    arriving = [first[0][2], first[1][2]]
     fetched[9].wait()
     fetched[10].wait()
 
@@ -334,27 +371,26 @@
     for offset in range(1, GROUP):
         arriving.append(
             send(
-                near_s.at[peer(offset)], table_o.at[pl.ds(LEAVES + me * SLOT, SLOT)],
+                near_s.at[peer(offset)], table_o.at[pl.ds(me * SLOT, SLOT)],
                 near_send.at[offset - 1], near_recv.at[offset - 1], member(peer(offset)),
             )
         )
     arriving.append(
         send(
-            side_buf.at[1], table_o.at[pl.ds(2 * LEAVES, HALO)],
+            side_buf.at[1], table_o.at[pl.ds(LEAVES, HALO)],
             near_send.at[7], near_recv.at[7], cousin(1),
         )
     )
     arriving.append(
         send(
-            side_buf.at[0], table_o.at[pl.ds(2 * LEAVES + HALO, HALO)],
+            side_buf.at[0], table_o.at[pl.ds(LEAVES + HALO, HALO)],
             near_send.at[8], near_recv.at[8], cousin(BRANCHES - 1),
         )
     )
-    keep(table_s, table_o.at[pl.ds(0, LEAVES)], local_sem.at[0])
-    keep(near_s.at[me], table_o.at[pl.ds(LEAVES + me * SLOT, SLOT)], local_sem.at[1])
-
-    rest_first = ring_first(1, pool_s.at[pl.ds(32, 32)])
-    arriving.append(rest_first[2])
+    keep(near_s.at[me], table_o.at[pl.ds(me * SLOT, SLOT)], local_sem.at[1])
+
+    first.append(ring_first(2))
+    arriving.append(first[2][2])
     keep(pool_s, pool_o.at[me], local_sem.at[2])
     keep(edges, edges_o, local_sem.at[4])
 
@@ -385,11 +421,11 @@
     high = roots_s[4] + roots_s[5] + roots_s[6] + roots_s[7]
     upper_s[0] = low
     upper_s[1] = high
-    first = dot(jnp.concatenate([low, high], axis=1), edges_up[0:256, :]).astype(BF)
-    upper_s[2] = first
-    second = dot(first, edges_up[256:384, :]).astype(BF)
-    third = dot(second[:, 0:64], edges_up[384:448, :]).astype(BF)
-    upper_s[3] = jnp.where(iota((16, 128), 1) < 64, second.astype(F32), third.astype(F32)).astype(BF)
+    level1 = dot(jnp.concatenate([low, high], axis=1), edges_up[0:256, :]).astype(BF)
+    upper_s[2] = level1
+    level2 = dot(level1, edges_up[256:384, :]).astype(BF)
+    level3 = dot(level2[:, 0:64], edges_up[384:448, :]).astype(BF)
+    upper_s[3] = jnp.where(left, level2.astype(F32), level3.astype(F32)).astype(BF)
 
     def spread_up(offset, carry):
         pltpu.make_async_remote_copy(
@@ -427,8 +463,8 @@
     codes[:, 0:254] = (partner[...] >> width) * 256 + start + (partner[...] & ((1 << width) - 1))
     keep(codes, codes_o, local_sem.at[6])
 
-    leaves_second = ring_second(0, leaves_first)
-    arriving += leaves_second[2:]
+    second = [ring_second(0, first[0]), ring_second(1, first[1])]
+    arriving += second[0][2:] + second[1][2:]
 
     fetched[7].wait()
     for f in range(FAR):
@@ -456,15 +492,43 @@
         )
         return carry
 
-    lax.fori_loop(0, 8, couple_rows, 0)
-    lax.fori_loop(8, 15, couple_rows, 0)
-    rest_second = ring_second(1, rest_first)
-    arriving += rest_second[2:]
+    lax.fori_loop(0, 15, couple_rows, 0)
     couple_one(lambda f, g: block_tail[f, :, 128 * g : 128 * g + 128], 7680, 0)
     keep(blocks, blocks_o, local_sem.at[7])
-
-    arriving += ring_third(0, leaves_second)
-    arriving += ring_third(1, rest_second)
+    second.append(ring_second(2, first[2]))
+    arriving += second[2][2:]
+
+    eye = (iota((128, 128), 0) == iota((128, 128), 1)).astype(F32).astype(BF)
+
+    def goals(c, carry):
+        lanes = pl.ds(pl.multiple_of(c * 128, 128), 128)
+        features = target_features(xyz[:, lanes].astype(F32)).astype(BF)
+        turned = dot_nt(eye, jnp.concatenate([features] * 4, axis=0)).astype(BF)
+        goals_s[2 * c] = turned[0:64]
+        goals_s[2 * c + 1] = turned[64:128]
+        return carry
+
+    lax.fori_loop(0, 64, goals, 0, unroll=16)
+    keep(goals_s, goals_o, local_sem.at[9])
+    swap_halves(table_s, swap_s, LEAVES)
+    fetched[11].wait()
+    fetched[12].wait()
+
+    def own_pairs(c, carry):
+        for k in range(16):
+            place = 64 * c + 4 * k
+            at = [jnp.minimum(source[0, RECEIVED + place + i], LEAVES - 1) for i in range(4)]
+            to = [target[0, RECEIVED + place + i] for i in range(4)]
+            for i, part in enumerate(near_quad(goals_s, table_s, swap_s, at, to, left)):
+                terms[place + i] = part.astype(BF)
+        return carry
+
+    for k, (start, stop) in enumerate(((0, 5), (5, 9), (9, 13))):
+        lax.fori_loop(start, stop, own_pairs, 0)
+        span = pl.ds(64 * start, 64 * (stop - start))
+        keep(terms.at[span], terms_o.at[span], local_sem.at[10 + k])
+        arriving += ring_third(k, second[k])
+
     cup_copy.wait_recv()
     cup_own[...] = cup_own[...] + cup_recv[...]
     keep(cup_own, cup_o, local_sem.at[8])
@@ -486,13 +550,13 @@
         copy.wait()
 
 
-def exchange(rhs, xyz, order, basis, trans, tup, cup, couple, partner, send_list, side_list):
+def exchange(rhs, xyz, order, basis, trans, tup, cup, couple, partner, send_list, side_list, target, source):
     shape = jax.ShapeDtypeStruct
-    inputs = (rhs, xyz, order, basis, trans, tup, cup, couple, partner, send_list, side_list)
+    inputs = (rhs, xyz, order, basis, trans, tup, cup, couple, partner, send_list, side_list, target, source)
     return pl.pallas_call(
         exchange_kernel,
         out_shape=(
-            shape((2 * LEAVES + 2 * HALO, 16, 128), BF),
+            shape((RECEIVED, 16, 128), BF),
             shape((GROUP, TILES, 16, 128), BF),
             shape((BRANCHES, 4, 16, 128), BF),
             shape((8192, 128), BF),
@@ -500,9 +564,11 @@
             shape((FAR, 8, 1024), F32),
             shape((8192, 256), BF),
             shape((FAR, 256), I32),
+            shape((LEAVES, 64, 64), BF),
+            shape((OWN, 16, 64), BF),
         ),
-        in_specs=[HBM] * 11,
-        out_specs=(HBM,) * 8,
+        in_specs=[HBM] * 13,
+        out_specs=(HBM,) * 10,
         scratch_shapes=[pltpu.VMEM(value.shape, value.dtype) for value in inputs[:9]]
         + [pltpu.SMEM(value.shape, value.dtype) for value in inputs[9:]]
         + [
@@ -525,10 +591,13 @@
             pltpu.VMEM((FAR, 16, 1024), F32),
             pltpu.VMEM((8192, 256), BF),
             pltpu.VMEM((FAR, 256), I32),
+            pltpu.VMEM((LEAVES, 64, 64), BF),
+            pltpu.VMEM((LEAVES, 16, 128), BF),
+            pltpu.VMEM((OWN, 16, 64), BF),
         ]
         + [
             pltpu.SemaphoreType.DMA((count,))
-            for count in (11, 9, 9, 10, 10, 8, 8, 7, 7, BRANCHES - 1, BRANCHES - 1, 2, 9)
+            for count in (13, 9, 9, 15, 15, 12, 12, 7, 7, BRANCHES - 1, BRANCHES - 1, 2, 13)
         ],
         compiler_params=pltpu.CompilerParams(
             collective_id=0, has_side_effects=True, vmem_limit_bytes=64 * 1024 * 1024
@@ -538,88 +607,60 @@
 
 
 def local_kernel(
-    table_h, target_h, source_h, count_h, xyz_h, pool_h, blocks_h, codes_h, upper_h, edges_up_h, cup_h, pup_h,
+    table_h, target_h, source_h, count_h, goals_h, terms_h, pool_h, blocks_h, codes_h, upper_h, edges_up_h, cup_h, pup_h,
     edges_h, basis_h, order_h,
     out,
-    table, target, source, count, xyz, pool, blocks, codes, upper, edges_up, cup, pup, edges, basis, order,
-    swap_s, goal_s, pool_rep, block_up, upper_s, coupled_s, local_s, near_s, sum_s, in_sem,
+    table, target, source, count, goals, terms, pool, blocks, codes, upper, edges_up, cup, pup, edges, basis, order,
+    swap_s, pool_rep, block_up, upper_s, coupled_s, local_s, near_s, sum_s, in_sem,
 ):
-    given = (table_h, target_h, source_h, count_h, xyz_h, pool_h, blocks_h, codes_h, upper_h, edges_up_h, cup_h, pup_h,
+    given = (table_h, target_h, source_h, count_h, goals_h, terms_h, pool_h, blocks_h, codes_h, upper_h, edges_up_h, cup_h, pup_h,
              edges_h, basis_h, order_h)
-    held = (table, target, source, count, xyz, pool, blocks, codes, upper, edges_up, cup, pup, edges, basis, order)
+    held = (table, target, source, count, goals, terms, pool, blocks, codes, upper, edges_up, cup, pup, edges, basis, order)
     fetched = [pltpu.make_async_copy(a, b, in_sem.at[i]) for i, (a, b) in enumerate(zip(given, held))]
-    for i in (4, 0, 1, 2, 3, 5, 6, 7, 8, 9, 10, 11, 12, 13, 14):
-        fetched[i].start()
-    fetched[4].wait()
+    for copy in fetched:
+        copy.start()
     branch = lax.axis_index("branch")
     me = lax.axis_index("row") * 2 + lax.axis_index("top")
     device = branch * GROUP + me
     left = iota((16, 128), 1) < 64
     lane_block = iota((16, 128), 1) >> 5
 
-    eye = (iota((128, 128), 0) == iota((128, 128), 1)).astype(F32).astype(BF)
-
-    def goals(c, carry):
-        lanes = pl.ds(pl.multiple_of(c * 128, 128), 128)
-        features = target_features(xyz[:, lanes].astype(F32)).astype(BF)
-        turned = dot_nt(eye, jnp.concatenate([features] * 4, axis=0)).astype(BF)
-        goal_s[2 * c] = turned[0:64]
-        goal_s[2 * c + 1] = turned[64:128]
-        return carry
-
-    lax.fori_loop(0, 64, goals, 0, unroll=16)
-
     def clear(t, carry):
         near_s[t] = jnp.zeros((16, 64), F32)
         return carry
 
     lax.fori_loop(0, LEAVES + 1, clear, 0, unroll=3)
 
-    for copy in fetched[:4]:
+    for copy in fetched[:5]:
         copy.wait()
-
-    def swaps(c, carry):
-        tiles = table[pl.ds(8 * c, 8)].reshape(128, 128).astype(F32)
-        swap_s[pl.ds(8 * c, 8)] = pltpu.roll(tiles, 64, 1).astype(BF).reshape(8, 16, 128)
-        return carry
-
-    lax.fori_loop(0, 40, swaps, 0, unroll=4)
-
-    live = count[0]
-    lane16 = (iota((64, 64), 1) >> 4)
+    swap_halves(table, swap_s, RECEIVED)
     zero = jnp.zeros((16, 128), BF)
-
-    def quad(first):
-        at = [source[0, first + i] for i in range(4)]
-        to = [target[0, first + i] for i in range(4)]
-        g = [goal_s[to[i]] for i in range(4)]
-        lhs = jnp.where(lane16 == 0, g[0], jnp.where(lane16 == 1, g[1], jnp.where(lane16 == 2, g[2], g[3])))
-        value, other = [], []
-        for i in range(4):
-            plain, swapped = table[at[i]], swap_s[at[i]]
-            if i % 2 == 0:
-                pieces = [jnp.where(left, plain, zero), jnp.where(left, swapped, zero)]
-            else:
-                pieces = [jnp.where(left, zero, swapped), jnp.where(left, zero, plain)]
-            for rows, piece in zip((value, other), pieces):
-                rows.append(jnp.concatenate([piece, zero] if i < 2 else [zero, piece], axis=1))
-        tile = lax.rsqrt(dot(lhs, jnp.concatenate(other, axis=0))).astype(BF)
-        wide = dot_nt(jnp.concatenate(value, axis=0), tile)
-        return [
-            (jnp.where(first + i < live, to[i], LEAVES), wide[16 * i : 16 * i + 16]) for i in range(4)
-        ]
 
     def near(c, carry):
         outs = []
         for k in range(16):
-            outs += quad(c * 64 + 4 * k)
+            place = 64 * c + 4 * k
+            at = [source[0, place + i] - LEAVES for i in range(4)]
+            to = [target[0, place + i] for i in range(4)]
+            outs += zip(to, near_quad(goals, table, swap_s, at, to, left))
         for goal, part in outs:
             near_s[goal] = near_s[goal] + part
         return carry
 
-    lax.fori_loop(0, (live + 63) // 64, near, 0)
-
-    for copy in fetched[5:12]:
+    lax.fori_loop(0, RECEIVED // 64, near, 0)
+    fetched[5].wait()
+    live = count[0] - RECEIVED
+
+    def add_terms(c, carry):
+        for k in range(16):
+            place = 16 * c + k
+            goal = jnp.where(place < live, target[0, RECEIVED + place], LEAVES)
+            near_s[goal] = near_s[goal] + terms[place].astype(F32)
+        return carry
+
+    lax.fori_loop(0, (live + 15) // 16, add_terms, 0)
+
+    for copy in fetched[6:13]:
         copy.wait()
 
     def put_up(a, low, high):
@@ -724,7 +765,7 @@
         step = dot_nt(current.astype(BF), jnp.concatenate([matrix] * 4, axis=0))
         current = everywhere(tiles[level // 4], level % 4) + step
 
-    for copy in fetched[12:]:
+    for copy in fetched[13:]:
         copy.wait()
     rows6 = first_row(6) * 32
     local_s[63] = coupled_s[63] + dot_nt(current.astype(BF), edges[rows6 : rows6 + 128, :])
@@ -773,20 +814,18 @@
         out[:, 256 * low : 256 * low + 256] = sum_s[16 * low : 16 * low + 16, :]
 
 
-def local(table, target, source, count, xyz, pool, blocks, codes, upper, edges_up, cup, pup, edges, basis, order):
-    inputs = (table, target, source, count, xyz, pool, blocks, codes, upper, edges_up, cup, pup, edges, basis, order)
-    scalars = (1, 2, 3, 7, 11)
+def local(*inputs):
+    scalars = (1, 2, 3, 8, 12)
     return pl.pallas_call(
         local_kernel,
         out_shape=jax.ShapeDtypeStruct((NRHS, POINTS), F32),
-        in_specs=[HBM] * 15,
+        in_specs=[HBM] * 16,
         out_specs=VMEM,
         scratch_shapes=[
             (pltpu.SMEM if i in scalars else pltpu.VMEM)(value.shape, value.dtype) for i, value in enumerate(inputs)
         ]
         + [
-            pltpu.VMEM((2 * LEAVES + 2 * HALO, 16, 128), BF),
-            pltpu.VMEM((LEAVES, 64, 64), BF),
+            pltpu.VMEM((RECEIVED, 16, 128), BF),
             pltpu.VMEM((GROUP * TILES, 4, 16, 128), BF),
             pltpu.VMEM((2, 256, 128), F32),
             pltpu.VMEM((14, 16, 128), BF),
@@ -794,7 +833,7 @@
             pltpu.VMEM((TILES, 16, 128), F32),
             pltpu.VMEM((LEAVES + 1, 16, 64), F32),
             pltpu.VMEM((512, 256), F32),
-            pltpu.SemaphoreType.DMA((15,)),
+            pltpu.SemaphoreType.DMA((16,)),
         ],
         compiler_params=pltpu.CompilerParams(vmem_limit_bytes=64 * 1024 * 1024),
         name="local",
@@ -819,12 +858,13 @@
     pair_count,
 ):
     order = point_order.reshape(1, POINTS)
-    table, pool, upper, edges, edges_up, cup, blocks, codes = exchange(
+    table, pool, upper, edges, edges_up, cup, blocks, codes, goals, terms = exchange(
         right_sides, positions, order, leaf_basis, transfer, transfer_up,
         couple_up.transpose(1, 0, 2), couple_local.transpose(1, 0, 2), partner_local.T, send_list[0], side_list[0],
+        pair_target, pair_source,
     )
     return local(
-        table, pair_target, pair_source, pair_count, positions, pool.reshape(GROUP * TILES, 16, 128), blocks, codes,
+        table, pair_target, pair_source, pair_count, goals, terms, pool.reshape(GROUP * TILES, 16, 128), blocks, codes,
         upper, edges_up, cup, partner_up.T, edges, leaf_basis, order,
     )
 

time: 67 us -> 64.2 us (0.958)
  Pallas kernels: 66.2 us -> 63.5 us
    pallas_call x1, Pallas kernels: 30.1 us -> 22.3 us  [local(): pl.pallas_call(local_kernel, out_shape=jax.ShapeDtypeStruct((NRHS, POINTS...]
    pallas_call x1, Pallas kernels: 36.2 us -> 41.2 us  [exchange(): pl.pallas_call(exchange_kernel, out_shape=(shape((RECEIVED, 16, 128), BF)...]
where the time goes in v3:
time: 64.2 us
  Pallas kernels  63.5 us (99%)
  between operations  0.66 us (1%)
    pallas_call x1, Pallas kernels, exchange(): pl.pallas_call(exchange_kernel, out_shape=(shape((RECEIVED, 16, 128), BF)...  41.2 us
    pallas_call x1, Pallas kernels, local(): pl.pallas_call(local_kernel, out_shape=jax.ShapeDtypeStruct((NRHS, POINTS...  22.3 us

profile of v3, /device:TPU:1, one launch (start us, length us, event | category | flops | bytes accessed | tf_op | source)
XLA Modules:
  0.0 64.2 jit_solution(7474991155728588764)
XLA Ops:
  0.7 41.2 %exchange.1 = (bf16[192,16,128]{2,1,0:T(8,128)(2,1)}, bf16[8,64,16,128]{3,2,1,0:T(8,128)(2,1)}, bf16[32,4,16,128]{3,2,1,0:T(8,128)(2,1)}, bf16[8192,128]{1,0:T(8...) custom-call(bf16[16,8192]{1,0:T(8,128)(2,1)} %rhs_h.1, ...), custom_call_target="tpu_custom_call" | custom-call | tf_op jit(solution)/shard_map/exchange/pallas_call | solution.py:556
  41.9 22.3 %local.1 = f32[16,8192]{1,0:T(8,128)} custom-call(bf16[192,16,128]{2,1,0:T(8,128)(2,1)} %get-tuple-element.15.table_h, s32[1,1024]{1,0:T(1,128)} %target_h.3, s32[1,1024]{1,0:T(1,128)} %source_h.3, s32[1]{0:T(128)S(6)} %copy.16.count_h, bf16[128,64,64]{2,1,0:T(8,128)(2,1)} %get-tuple-element.16.goals_h, bf16[832,16,64]{2,1,0:T(8,128)(2,1)} %get-tuple-element.17.terms_h, ...), custom_call_target="tpu_custom_call" | custom-call | tf_op jit(solution)/shard_map/local/pallas_call | solution.py:819

commit v4 on v3

--- a/solution.py
+++ b/solution.py
@@ -485,14 +485,15 @@
                 ].astype(BF)
 
     def couple_rows(c, carry):
-        start = pl.multiple_of(16 * c, 16)
-        couple_one(
-            lambda f, g: couple[f, pl.ds(start, 16), 128 * g : 128 * g + 128].astype(F32),
-            512 * c, 0,
-        )
-        return carry
-
-    lax.fori_loop(0, 15, couple_rows, 0)
+        for part in range(3):
+            start = pl.multiple_of(48 * c + 16 * part, 16)
+            couple_one(
+                lambda f, g: couple[f, pl.ds(start, 16), 128 * g : 128 * g + 128].astype(F32),
+                1536 * c + 512 * part, part,
+            )
+        return carry
+
+    lax.fori_loop(0, 5, couple_rows, 0)
     couple_one(lambda f, g: block_tail[f, :, 128 * g : 128 * g + 128], 7680, 0)
     keep(blocks, blocks_o, local_sem.at[7])
     second.append(ring_second(2, first[2]))
@@ -587,7 +588,7 @@
             pltpu.VMEM((FAR, 8, 1024), F32),
             pltpu.VMEM((8192, 128), BF),
             pltpu.VMEM((2048, 128), BF),
-            pltpu.VMEM((1, 2, 16 * PITCH, 128), F32),
+            pltpu.VMEM((3, 2, 16 * PITCH, 128), F32),
             pltpu.VMEM((FAR, 16, 1024), F32),
             pltpu.VMEM((8192, 256), BF),
             pltpu.VMEM((FAR, 256), I32),

time: 64.2 us -> 64.2 us (level)
  no operation moved by 1% of the time
where the time goes in v4:
time: 64.2 us; the launch traced here: 64.1 us
  Pallas kernels  63.5 us (99%)
  between operations  0.66 us (1%)
    pallas_call x1, Pallas kernels, exchange(): pl.pallas_call(exchange_kernel, out_shape=(shape((RECEIVED, 16, 128), BF)...  41.2 us
    pallas_call x1, Pallas kernels, local(): pl.pallas_call(local_kernel, out_shape=jax.ShapeDtypeStruct((NRHS, POINTS...  22.3 us

profile of v4, /device:TPU:1, one launch (start us, length us, event | category | flops | bytes accessed | tf_op | source)
XLA Modules:
  0.0 64.1 jit_solution(18197100488572991685)
XLA Ops:
  0.7 41.2 %exchange.1 = (bf16[192,16,128]{2,1,0:T(8,128)(2,1)}, bf16[8,64,16,128]{3,2,1,0:T(8,128)(2,1)}, bf16[32,4,16,128]{3,2,1,0:T(8,128)(2,1)}, bf16[8192,128]{1,0:T(8...) custom-call(bf16[16,8192]{1,0:T(8,128)(2,1)} %rhs_h.1, ...), custom_call_target="tpu_custom_call" | custom-call | tf_op jit(solution)/shard_map/exchange/pallas_call | solution.py:557
  41.9 22.3 %local.1 = f32[16,8192]{1,0:T(8,128)} custom-call(bf16[192,16,128]{2,1,0:T(8,128)(2,1)} %get-tuple-element.15.table_h, s32[1,1024]{1,0:T(1,128)} %target_h.3, s32[1,1024]{1,0:T(1,128)} %source_h.3, s32[1]{0:T(128)S(6)} %copy.16.count_h, bf16[128,64,64]{2,1,0:T(8,128)(2,1)} %get-tuple-element.16.goals_h, bf16[832,16,64]{2,1,0:T(8,128)(2,1)} %get-tuple-element.17.terms_h, ...), custom_call_target="tpu_custom_call" | custom-call | tf_op jit(solution)/shard_map/local/pallas_call | solution.py:820
